TPU v7x, 256 devices: a whole 4x4x8 slice. The times are simulated.
256 devices in a mesh: tok: 32 (over z, x), voc: 8 (over y, core).
Axes of the slice: x: 4, y: 4, z: 8, core: 2. Of those that a mesh axis runs over, the one named last changes fastest.
Arguments:
- hidden_states: bfloat16 [4096, 4096], P('tok', 'voc'), may hold values from -20 to 20
- head: bfloat16 [4096, 65536], P('voc', 'tok'), may hold values from -0.0625 to 0.0625
- proj_in: bfloat16 [4096, 128], P('voc'), may hold values from -0.09375 to 0.09375
- proj_out: bfloat16 [65536, 128], P('tok'), may hold values from -6 to 6
- targets: int32 [4096], P('voc'), may hold values from 0 to 65535
- lengths: int32 [8, 8], P('voc'), may hold values from 1 to 256, 512 in all within a row
Outputs:
- attributions: float32 [64, 128, 128], P('voc', 'tok')
Inputs may be any that keep to these rules, and one draw needn't show every extreme that they name: The lengths of each sequence add up to 512.
All inputs are finite; a program needn't handle non-finite values.
Results may differ from a plain program's by a relative error of at most 0.0031.
Values may be sent and summed in bfloat16 or wider, within the bound.
No kernel may reach another device: no remote copies, remote signals or barrier semaphores. Data moves between devices by JAX's collectives and lax.ppermute only.
A program may use at most 128 MiB of HBM per device.

v0:
```python
import jax
import jax.numpy as jnp
from jax import lax
from jax.sharding import PartitionSpec as P


def local(hidden_states, head, proj_in, proj_out, targets, lengths):
    slice_cols = head.shape[1]
    seq_count = targets.shape[0]
    in_width = proj_in.shape[1]
    everyone = lax.all_gather(hidden_states, "tok", axis=0, tiled=True)
    joined = jnp.concatenate([head, proj_in], axis=1)
    summed = lax.psum_scatter(
        jnp.dot(everyone, joined, preferred_element_type=jnp.float32),
        "voc",
        scatter_dimension=0,
        tiled=True,
    )
    logits = summed[:, :slice_cols]
    in_proj = summed[:, slice_cols:].astype(jnp.bfloat16)
    local_max = jnp.max(logits, axis=1)
    row_max = lax.pmax(local_max, "tok")
    shifted = jnp.exp(logits - row_max[:, None])
    row_total = lax.psum(jnp.sum(shifted, axis=1), "tok")
    offset = lax.axis_index("tok") * slice_cols
    columns = offset + jnp.arange(slice_cols, dtype=jnp.int32)
    onehot = (targets[:, None] == columns[None, :]).astype(jnp.float32)
    grad_logits = (shifted / row_total[:, None] - onehot).astype(jnp.bfloat16)
    partial_out = jnp.dot(grad_logits, proj_out, preferred_element_type=jnp.float32)
    seq_lengths = lengths[0]
    ends = jnp.cumsum(seq_lengths)
    starts = ends - seq_lengths
    positions = jnp.arange(seq_count, dtype=jnp.int32)
    member = (
        (positions[:, None] >= starts[None, :]) & (positions[:, None] < ends[None, :])
    ).astype(jnp.float32)
    membership = member / seq_lengths.astype(jnp.float32)[None, :]
    out_proj = lax.psum(partial_out, "tok")
    own_rows = in_width // lax.axis_size("tok")
    row_start = lax.axis_index("tok") * own_rows
    in_slice = lax.dynamic_slice_in_dim(in_proj, row_start, own_rows, 1)
    expanded = membership[:, :, None] * in_slice.astype(jnp.float32)[:, None, :]
    return jnp.einsum("ter,tc->erc", expanded, out_proj, precision=lax.Precision.HIGHEST)


def solution(mesh):
    placed = (
        P("tok", "voc"),
        P("voc", "tok"),
        P("voc", None),
        P("tok", None),
        P("voc"),
        P("voc", None),
    )
    return jax.shard_map(
        local, mesh=mesh, in_specs=placed, out_specs=P("voc", "tok", None), check_vma=False
    )
```

profile of v0, /device:TPU:8, one launch (start us, length us, event | category | flops | bytes accessed | tf_op | source)
XLA Modules:
  0.0 595.1 jit_solution(8342531669830420824)
XLA Ops:
  6.5 0.0 copy-start
  6.5 0.0 all-gather.2.cloned.1.call-start
  6.5 0.7 all-gather.2.cloned.1.call-update
  7.3 0.0 reduce-scatter.2.cloned.1.call-start
  7.3 87.3 %all-gather.2.cloned.1.call-done = bf16[4096,512]{1,0:T(8,128)(2,1)} async-done(((bf16[128,512]{1,0:T(8,128)(2,1)}), bf16[4096,512]{1,0:T(8,128)(2,1)}) %all-gather.2.cloned.1.call-update) | async-done | bytes 4194320 | tf_op jit(solution)/shard_map/all_gather | solution.py:11
  94.6 18.4 %convolution_bitcast_fusion = f32[4096,2176]{0,1:T(8,128)} fusion(bf16[4096,512]{1,0:T(8,128)(2,1)} %all-gather.2.cloned.1.call-done, bf16[512,128]{1,0:T(8,128)(2,1)} %param.8, bf16[512,2048]{1,0:T(8,128)(2,1)} %param.7), kind=kOutput, calls=%fused_computation | convolution fusion | flops 9131261952 | bytes 42074112 | tf_op jit(solution)/shard_map/dot_general | solution.py:14
  113.1 0.0 copy-start.1
  113.1 0.0 reduce-scatter.2.cloned.1.call-update
  113.1 0.0 all-reduce.2.cloned.1.call-start
  113.2 0.6 copy-done.1
  113.7 0.2 reduce-window.4
  113.9 0.0 copy-start.2
  113.9 177.1 %reduce-scatter.2.cloned.1.call-done = f32[512,2176]{0,1:T(8,128)} async-done(((f32[4096,2176]{0,1:T(8,128)}), f32[512,2176]{0,1:T(8,128)}) %reduce-scatter.2.cloned.1.call-update) | async-done | bytes 4456464 | tf_op jit(solution)/shard_map/reduce_scatter | solution.py:13
  291.0 2.5 slice_reduce_fusion
  293.5 75.3 %pmax.7 = f32[512]{0:T(512)S(1)} all-reduce(f32[512]{0:T(512)S(1)} %slice_reduce_fusion), channel_id=1, replica_groups=mesh['tok'=32,'voc'=8] {'tok'}, use_global_device_ids=true, to_apply=%region_3.0 | all-reduce | flops 512 | bytes 4096 | tf_op jit(solution)/shard_map/pmax | solution.py:22
  368.8 2.8 fusion
  371.7 69.6 %psum.14 = f32[512]{0:T(512)S(1)} all-reduce(f32[512]{0:T(512)S(1)} %fusion), channel_id=1, replica_groups=mesh['tok'=32,'voc'=8] {'tok'}, use_global_device_ids=true, to_apply=%region_5.0 | all-reduce | flops 512 | bytes 4096 | tf_op jit(solution)/shard_map/psum | solution.py:24
  441.3 0.0 copy-done
  441.3 0.0 copy-done.2
  441.3 3.8 fusion.4
  445.1 0.0 all-reduce.2.cloned.1.call-update
  445.1 0.1 convert_divide_fusion
  445.2 1.0 slice.9
  446.2 140.6 %all-reduce.2.cloned.1.call-done = f32[512,128]{1,0:T(8,128)} async-done(((f32[512,128]{1,0:T(8,128)}), f32[512,128]{1,0:T(8,128)}) %all-reduce.2.cloned.1.call-update) | async-done | bytes 262160 | tf_op jit(solution)/shard_map/psum | solution.py:38
  586.8 1.2 fusion.5
  588.0 0.6 copy.7
  (3 shorter events, 0.0 us)
Async XLA Ops:
  6.5 434.7 %copy-start = (bf16[2048,128]{1,0:T(8,128)(2,1)S(1)}, bf16[2048,128]{1,0:T(8,128)(2,1)}, u32[]{:S(2)}) copy-start(bf16[2048,128]{1,0:T(8,128)(2,1)} %param.9) | copy-start | bytes 1572868
  6.5 88.1 %all-gather.2.cloned.1.call-start = ((), (), s32[]{:S(2)}) async-start(), calls=%async_computation.1 | async-start | bytes 4325376 | tf_op jit(solution)/shard_map/all_gather | solution.py:11
  7.3 283.8 %reduce-scatter.2.cloned.1.call-start = ((), (), s32[]{:S(2)}) async-start(), calls=%async_computation.2 | async-start | bytes 40108032 | tf_op jit(solution)/shard_map/reduce_scatter | solution.py:13
  113.1 0.7 copy-start.1
  113.1 473.7 %all-reduce.2.cloned.1.call-start = ((), (), s32[]{:S(2)}) async-start(), calls=%async_computation.3 | async-start | bytes 524288 | tf_op jit(solution)/shard_map/psum | solution.py:38
  113.9 327.4 %copy-start.2 = (s32[512]{0:T(512)S(1)}, s32[512]{0:T(512)}, u32[]{:S(2)}) copy-start(s32[512]{0:T(512)} %param.10) | copy-start | bytes 6148
Sparse Core Ops, SparseCore 0:
  9.9 84.6 all-gather.1
  113.2 177.7 reduce-scatter.1
  445.2 141.4 all-reduce.1
where the time goes:
time: 595 us
  waiting for transfers between devices  406 us (68%)
  blocking collectives  145 us (24%)
  matrix products  23.5 us (4%)
  between operations  13.1 us (2%)
    reduce_scatter x1, waiting for transfers between devices, local(): lax.psum_scatter(jnp.dot(everyone, joined, preferred_element_type=jnp.flo...  177 us
    psum x1, waiting for transfers between devices, local(): out_proj = lax.psum(partial_out, 'tok')  141 us
    all_gather x1, waiting for transfers between devices, local(): everyone = lax.all_gather(hidden_states, 'tok', axis=0, tiled=True)  87.3 us
    pmax x1, blocking collectives, local(): row_max = lax.pmax(local_max, 'tok')  75.3 us
    psum x1, blocking collectives, local(): row_total = lax.psum(jnp.sum(shifted, axis=1), 'tok')  69.6 us
    dot_general x1, matrix products, local(): jnp.dot(everyone, joined, preferred_element_type=jnp.float32)  18.4 us
  transfers between devices with their start and end apart: 3, of which 3 were waited for; matrix products, arithmetic and copies ran while one was open for 0% of the time, Pallas kernels for 0%

commit v1 on v0

v1 whole, which is shorter than its diff:
```python
import functools

import jax
import jax.numpy as jnp
from jax import lax
from jax.experimental import pallas as pl
from jax.experimental.pallas import tpu as pltpu
from jax.sharding import Mesh, PartitionSpec as P

TILE = 512
F32 = jnp.float32
BF16 = jnp.bfloat16


def shift(x, axis, by):
    n = lax.axis_size(axis)
    return lax.ppermute(x, axis, [(i, (i + by) % n) for i in range(n)])


def swap(x):
    return shift(x, "c", 1)


def exchange_corners(x):
    pairs = []
    for z in range(8):
        for xx in range(4):
            for v in range(8):
                src = (z * 4 + xx) * 8 + v
                dst = (v * 4 + xx) * 8 + z
                pairs.append((src, dst))
    return lax.ppermute(x, ("z", "x", "y", "c"), pairs)


def gather_hidden(block):
    z = lax.axis_index("z")
    x = lax.axis_index("x")
    mine = jnp.zeros((512, 512), BF16)
    for by in (0, 1, 3, 2):
        got = block if by == 0 else shift(block, "x", by)
        mine = lax.dynamic_update_slice(mine, got, (((x - by) % 4) * 128, 0))
    stack = jnp.zeros((8, 512, 512), BF16)

    def put(stack, piece, slot, row=0):
        return lax.dynamic_update_slice(stack, piece[None], (slot % 8, row, 0))

    stack = put(stack, mine, z)
    right, left = mine, mine
    for step in (1, 2, 3):
        right = shift(right, "z", 1)
        left = shift(left, "z", -1)
        stack = put(stack, right, z - step)
        stack = put(stack, left, z + step)
    far_a = shift(right[:256], "z", 1)
    far_b = shift(left[256:], "z", -1)
    stack = put(stack, far_a, z + 4, 0)
    return put(stack, far_b, z + 4, 256)


def dots(hid_ref, slot_ref, pieces, refs, acc):
    for ref, (place, low, rows) in zip(refs, pieces):
        acc_part = jnp.dot(
            hid_ref[slot_ref[place], :, low : low + rows], ref[...], preferred_element_type=F32
        )
        acc = acc_part if acc is None else acc + acc_part
    return acc


def first_kernel(pieces, slot_ref, hid_ref, pin_ref, *refs):
    heads, (part_ref, in_ref) = refs[: len(pieces)], refs[len(pieces) :]

    @pl.when(pl.program_id(0) == 0)
    def _():
        acc = jnp.dot(hid_ref[0], pin_ref[0], preferred_element_type=F32)
        for d in range(1, 8):
            acc = acc + jnp.dot(hid_ref[d], pin_ref[d], preferred_element_type=F32)
        in_ref[...] = acc.astype(BF16)

    part_ref[...] = dots(hid_ref, slot_ref, pieces, heads, None)


def last_kernel(pieces, slot_ref, hid_ref, part_ref, proj_ref, tgt_ref, *refs):
    heads, (out_ref, max_ref, rest_ref, hit_ref, sum_ref) = refs[: len(pieces)], refs[len(pieces) :]
    step = pl.program_id(0)

    @pl.when(step == 0)
    def _():
        max_ref[...] = jnp.full_like(max_ref, -jnp.inf)
        rest_ref[...] = jnp.zeros_like(rest_ref)
        hit_ref[...] = jnp.zeros_like(hit_ref)
        sum_ref[...] = jnp.zeros_like(sum_ref)

    logits = dots(hid_ref, slot_ref, pieces, heads, part_ref[...])
    old = max_ref[...]
    new = jnp.maximum(old, jnp.max(logits, axis=1, keepdims=True))
    scale = jnp.exp(old - new)
    shifted = jnp.exp(logits - new)
    columns = lax.broadcasted_iota(jnp.int32, logits.shape, 1) + step * TILE
    at_target = columns == tgt_ref[...]
    rest = jnp.where(at_target, 0.0, shifted)
    hit = jnp.where(at_target, shifted, 0.0)
    max_ref[...] = new
    rest_ref[...] = rest_ref[...] * scale + jnp.sum(rest, axis=1, keepdims=True)
    hit_ref[...] = hit_ref[...] * scale + jnp.sum(hit, axis=1, keepdims=True)
    sum_ref[...] = sum_ref[...] * scale + jnp.dot(
        rest.astype(BF16), proj_ref[...], preferred_element_type=F32
    )

    @pl.when(step == pl.num_programs(0) - 1)
    def _():
        out_ref[:, :128] = sum_ref[...]
        lane = lax.broadcasted_iota(jnp.int32, (512, 128), 1)
        stats = jnp.where(lane == 0, max_ref[...], jnp.where(lane == 1, rest_ref[...], hit_ref[...]))
        out_ref[:, 128:] = stats


def merge_kernel(got_ref, rows_ref, out_ref):
    stats = got_ref[:, :, 128:]
    top = jnp.max(stats[:, :, 0:1], axis=0, keepdims=True)
    weight = jnp.exp(stats[:, :, 0:1] - top)
    rest = jnp.sum(weight * stats[:, :, 1:2], axis=0)
    hit = jnp.sum(weight * stats[:, :, 2:3], axis=0)
    total = jnp.sum(weight * got_ref[:, :, :128], axis=0)
    row = jnp.sum(rows_ref[...].astype(F32), axis=0)
    merged = (total - rest * row) / (rest + hit)
    out_ref[...] = jnp.broadcast_to(merged[None], out_ref.shape)


PARAMS = dict(dimension_semantics=("arbitrary",), vmem_limit_bytes=48 << 20)


def head_spec(ref):
    return pl.BlockSpec((ref.shape[0], TILE), lambda i, s: (0, i))


def whole(shape):
    return pl.BlockSpec(shape, lambda i, s: (0,) * len(shape))


def local(hidden_states, head, proj_in, proj_out, targets, lengths):
    z, x, y, c = (lax.axis_index(a) for a in ("z", "x", "y", "c"))
    me = z * 4 + x

    local_target = targets[:, None] - me * 2048
    onehot = (local_target == jnp.arange(2048, dtype=jnp.int32)[None, :]).astype(BF16)
    rows = jnp.dot(onehot, proj_out, preferred_element_type=F32).astype(BF16)
    rows = lax.all_to_all(rows, ("z", "x"), 0, 0, tiled=True).reshape(32, 16, 128)

    stack = gather_hidden(exchange_corners(hidden_states))
    pin = lax.all_gather(proj_in, ("y", "c"), axis=0, tiled=False).reshape(8, 512, 128)

    top, bottom = head[:256], head[256:]
    up_a, down_b = shift(top, "y", 1), shift(bottom, "y", -1)
    up_b, down_a = shift(bottom, "y", 1), shift(top, "y", -1)
    far_a, far_b = shift(up_a, "y", 1), shift(down_b, "y", -1)

    def slot(dy, dc):
        return ((y + dy) % 4) * 2 + (c + dc) % 2

    near = [(head, 0, 0, 512), (up_a, 1, 0, 256), (up_b, 1, 256, 256), (down_a, 2, 0, 256), (down_b, 2, 256, 256)]
    far = [(far_a, 0, 0, 256), (far_b, 0, 256, 256)]

    def both(items, count):
        refs = [i[0] for i in items] + [swap(i[0]) for i in items]
        pieces = [i[1:] for i in items] + [(i[1] + count, i[2], i[3]) for i in items]
        return refs, pieces

    near_refs, near_pieces = both(near, 3)
    far_refs, far_pieces = both(far, 1)
    near_slots = jnp.stack([slot(dy, dc) for dc in (0, 1) for dy in (0, -1, 1)]).astype(jnp.int32)
    far_slots = jnp.stack([slot(2, dc) for dc in (0, 1)]).astype(jnp.int32)

    flops = 2 * 512 * 2048
    part, in_proj = pl.pallas_call(
        functools.partial(first_kernel, near_pieces),
        out_shape=(jax.ShapeDtypeStruct((512, 2048), F32), jax.ShapeDtypeStruct((512, 128), BF16)),
        grid_spec=pltpu.PrefetchScalarGridSpec(
            num_scalar_prefetch=1,
            grid=(2048 // TILE,),
            in_specs=[whole((8, 512, 512)), whole((8, 512, 128))] + [head_spec(r) for r in near_refs],
            out_specs=(pl.BlockSpec((512, TILE), lambda i, s: (0, i)), whole((512, 128))),
        ),
        compiler_params=pltpu.CompilerParams(**PARAMS),
        cost_estimate=pl.CostEstimate(flops=flops * 3072, bytes_accessed=20 << 20, transcendentals=0),
        name="first_slices",
    )(near_slots, stack, pin, *near_refs)

    out = pl.pallas_call(
        functools.partial(last_kernel, far_pieces),
        out_shape=jax.ShapeDtypeStruct((512, 256), F32),
        grid_spec=pltpu.PrefetchScalarGridSpec(
            num_scalar_prefetch=1,
            grid=(2048 // TILE,),
            in_specs=[
                whole((8, 512, 512)),
                pl.BlockSpec((512, TILE), lambda i, s: (0, i)),
                pl.BlockSpec((TILE, 128), lambda i, s: (i, 0)),
                whole((512, 1)),
            ]
            + [head_spec(r) for r in far_refs],
            out_specs=whole((512, 256)),
            scratch_shapes=[pltpu.VMEM((512, 1), F32)] * 3 + [pltpu.VMEM((512, 128), F32)],
        ),
        compiler_params=pltpu.CompilerParams(**PARAMS),
        cost_estimate=pl.CostEstimate(flops=flops * 1152, bytes_accessed=14 << 20, transcendentals=1 << 20),
        name="last_slices",
    )(far_slots, stack, part, proj_out, local_target, *far_refs)

    got = lax.all_to_all(out, ("z", "x"), 0, 0, tiled=True).reshape(32, 16, 256)
    merged = pl.pallas_call(
        merge_kernel,
        out_shape=jax.ShapeDtypeStruct((32, 16, 128), F32),
        name="merge",
    )(got, rows)
    out_proj = lax.all_to_all(merged, ("z", "x"), 0, 0, tiled=True).reshape(512, 128)

    seq_lengths = lengths[0]
    ends = jnp.cumsum(seq_lengths)
    starts = ends - seq_lengths
    positions = jnp.arange(512, dtype=jnp.int32)
    member = (
        (positions[:, None] >= starts[None, :]) & (positions[:, None] < ends[None, :])
    ).astype(F32)
    membership = member / seq_lengths.astype(F32)[None, :]
    in_slice = lax.dynamic_slice_in_dim(in_proj, me * 4, 4, 1)
    expanded = membership[:, :, None] * in_slice.astype(F32)[:, None, :]
    return jnp.einsum("ter,tc->erc", expanded, out_proj, precision=lax.Precision.HIGHEST)


def solution(mesh):
    fine = Mesh(mesh.devices.reshape(8, 4, 4, 2), ("z", "x", "y", "c"))
    tok, voc = ("z", "x"), ("y", "c")
    placed = (P(tok, voc), P(voc, tok), P(voc, None), P(tok, None), P(voc), P(voc, None))
    return jax.shard_map(
        local, mesh=fine, in_specs=placed, out_specs=P(voc, tok, None), check_vma=False
    )
```

time: 595 us -> 224 us (0.38)
  waiting for transfers between devices: 406 us -> 94.6 us
  blocking collectives: 145 us -> 0 us
  starting transfers between devices: 0.08 us -> 59.3 us
  Pallas kernels: 0 us -> 27 us
  local copies, waits for them, and re-layouts: 2.17 us -> 26.6 us
  matrix products: 23.5 us -> 1.76 us
    reduce_scatter x1 -> x0, waiting for transfers between devices: 177 us -> none  [local(): lax.psum_scatter(jnp.dot(everyone, joined, preferred_element_type=jnp.flo...]
    psum x1 -> x0, waiting for transfers between devices: 141 us -> none  [local(): out_proj = lax.psum(partial_out, 'tok')]
    all_gather x1, waiting for transfers between devices: 87.3 us -> 0.01 us  [local(): lax.all_gather(proj_in, ('y', 'c'), axis=0, tiled=False)]
    pmax x1 -> x0, blocking collectives: 75.3 us -> none  [local(): row_max = lax.pmax(local_max, 'tok')]
    psum x1 -> x0, blocking collectives: 69.6 us -> none  [local(): row_total = lax.psum(jnp.sum(shifted, axis=1), 'tok')]
    ppermute x0 -> x25, waiting for transfers between devices: none -> 64.3 us  [the longest x24 53.6 us: shift(): return lax.ppermute(x, axis, [(i, (i + by) % n) for i in range(n)])]
    ppermute x0 -> x25, starting transfers between devices: none -> 40.1 us  [the longest x24 34.9 us: shift(): return lax.ppermute(x, axis, [(i, (i + by) % n) for i in range(n)])]
    all_to_all x0 -> x3, waiting for transfers between devices: none -> 30.2 us  [the longest x1 18.2 us: local(): got = lax.all_to_all(out, ('z', 'x'), 0, 0, tiled=True).reshape(32, 16, 256)]
  transfers between devices with their start and end apart: 3 -> 29, of which waited for: 3 -> 16; matrix products, arithmetic and copies ran while one was open for 0% -> 10% of each run, Pallas kernels for 0% -> 11%
where the time goes in v1:
time: 224 us; the launch traced here: 223 us
  waiting for transfers between devices  94.6 us (42%)
  starting transfers between devices  59.3 us (26%)
  Pallas kernels  27 us (12%)
  local copies, waits for them, and re-layouts  26.6 us (12%)
  between operations  13.8 us (6%)
    ppermute x24, waiting for transfers between devices, shift(): return lax.ppermute(x, axis, [(i, (i + by) % n) for i in range(n)])  53.6 us
    ppermute x24, starting transfers between devices, shift(): return lax.ppermute(x, axis, [(i, (i + by) % n) for i in range(n)])  34.9 us
    all_to_all x1, waiting for transfers between devices, local(): got = lax.all_to_all(out, ('z', 'x'), 0, 0, tiled=True).reshape(32, 16, 256)  18.2 us
    dynamic_update_slice x9, local copies, waits for them, and re-layouts, put(): return lax.dynamic_update_slice(stack, piece[None], (slot % 8, row, 0))  13.6 us
    pallas_call x1, Pallas kernels, local(): pl.pallas_call(functools.partial(first_kernel, near_pieces), out_shape=(j...  13.4 us
    all_to_all x1, waiting for transfers between devices, local(): lax.all_to_all(merged, ('z', 'x'), 0, 0, tiled=True).reshape(512, 128)  12 us
    pallas_call x1, Pallas kernels, local(): pl.pallas_call(functools.partial(last_kernel, far_pieces), out_shape=jax....  11.5 us
    ppermute x1, waiting for transfers between devices, exchange_corners(): return lax.ppermute(x, ('z', 'x', 'y', 'c'), pairs)  10.7 us
  transfers between devices with their start and end apart: 29, of which 16 were waited for; matrix products, arithmetic and copies ran while one was open for 10% of the time, Pallas kernels for 11%

profile of v1, /device:TPU:8, one launch (start us, length us, event | category | flops | bytes accessed | tf_op | source)
XLA Modules:
  0.0 223.5 jit_solution(12742146227241499306)
XLA Ops:
  6.5 5.2 %collective-permute-start = (bf16[128,512]{1,0:T(8,128)(2,1)}, bf16[128,512]{1,0:T(8,128)(2,1)S(1)}, u32[]{:S(2)}, u32[]{:S(2)}) collective-permute-start(bf16[128,512]{1,0:T(8,128)(2,1)} %param.6), channel_id=1, source_target_pairs={{0,0},{1,32},{2,64},{3,96},{4,128},{5,160},{6,192},{7,224},{8,8},{... | collective-permute-start | bytes 393224 | tf_op jit(solution)/shard_map/ppermute | solution.py:32
  11.7 10.7 %collective-permute-done = bf16[128,512]{1,0:T(8,128)(2,1)S(1)} collective-permute-done((bf16[128,512]{1,0:T(8,128)(2,1)}, bf16[128,512]{1,0:T(8,128)(2,1)S(1)}, u32[]{:S(2)}, u32[]{:S(2)}) %collective-permute-start) | collective-permute-done | bytes 131104 | tf_op jit(solution)/shard_map/ppermute | solution.py:32
  28.9 3.2 %collective-permute-done.3 = bf16[128,512]{1,0:T(8,128)(2,1)S(1)} collective-permute-done((bf16[128,512]{1,0:T(8,128)(2,1)S(1)}, bf16[128,512]{1,0:T(8,128)(2,1)S(1)}, u32[]{:S(2)}, u32[]{:S(2)}) %collective-permute-start.3) | collective-permute-done | bytes 131104 | tf_op jit(solution)/shard_map/ppermute | solution.py:17
  32.7 3.1 %fusion.9 = (bf16[256,2048]{1,0:T(8,128)(2,1)}, bf16[256,2048]{1,0:T(8,128)(2,1)}) fusion(bf16[512,2048]{1,0:T(8,128)(2,1)} %refs_0_.1), kind=kLoop, calls=%fused_computation.31 | loop fusion | bytes 4194304 | tf_op jit(solution)/shard_map/slice | solution.py:152
  36.6 4.6 %collective-permute-start.13 = (bf16[256,2048]{1,0:T(8,128)(2,1)}, bf16[256,2048]{1,0:T(8,128)(2,1)S(1)}, u32[]{:S(2)}, u32[]{:S(2)}) collective-permute-start(bf16[256,2048]{1,0:T(8,128)(2,1)} %get-tuple-element.9), channel_id=1, source_target_pairs={{0,2},{2,4},{4,6},{6,0},{1,3},{3,5},{5,7},{7,1},{8,10},{10,12},{12... | collective-permute-start | bytes 3145736 | tf_op jit(solution)/shard_map/ppermute | solution.py:17
  41.2 2.6 %collective-permute-start.5 = (bf16[512,512]{1,0:T(8,128)(2,1)S(1)}, bf16[512,512]{1,0:T(8,128)(2,1)}, u32[]{:S(2)}, u32[]{:S(2)}) collective-permute-start(bf16[512,512]{1,0:T(8,128)(2,1)S(1)} %constant_dynamic-update-slice_fusion), channel_id=1, source_target_pairs={{0,224},{32,0},{64,32},{96,64},{128,96},{160,128},{192,160},{224,1... | collective-permute-start | bytes 1572872 | tf_op jit(solution)/shard_map/ppermute | solution.py:17
  43.7 2.9 %collective-permute-done.4 = bf16[512,512]{1,0:T(8,128)(2,1)} collective-permute-done((bf16[512,512]{1,0:T(8,128)(2,1)S(1)}, bf16[512,512]{1,0:T(8,128)(2,1)}, u32[]{:S(2)}, u32[]{:S(2)}) %collective-permute-start.4) | collective-permute-done | bytes 524320 | tf_op jit(solution)/shard_map/ppermute | solution.py:17
  46.6 7.8 %collective-permute-done.5 = bf16[512,512]{1,0:T(8,128)(2,1)} collective-permute-done((bf16[512,512]{1,0:T(8,128)(2,1)S(1)}, bf16[512,512]{1,0:T(8,128)(2,1)}, u32[]{:S(2)}, u32[]{:S(2)}) %collective-permute-start.5) | collective-permute-done | bytes 524320 | tf_op jit(solution)/shard_map/ppermute | solution.py:17
  54.4 3.5 %collective-permute-start.7 = (bf16[512,512]{1,0:T(8,128)(2,1)}, bf16[512,512]{1,0:T(8,128)(2,1)}, u32[]{:S(2)}, u32[]{:S(2)}) collective-permute-start(bf16[512,512]{1,0:T(8,128)(2,1)} %collective-permute-done.5), channel_id=1, source_target_pairs={{0,224},{32,0},{64,32},{96,64},{128,96},{160,128},{192,160},{224,1... | collective-permute-start | bytes 1572872 | tf_op jit(solution)/shard_map/ppermute | solution.py:17
  59.7 2.5 %collective-permute-done.12.refs_1_ = bf16[256,2048]{1,0:T(8,128)(2,1)S(1)} collective-permute-done((bf16[256,2048]{1,0:T(8,128)(2,1)}, bf16[256,2048]{1,0:T(8,128)(2,1)S(1)}, u32[]{:S(2)}, u32[]{:S(2)}) %collective-permute-start.12) | collective-permute-done | bytes 1048608 | tf_op jit(solution)/shard_map/ppermute | solution.py:17
  62.2 3.8 %collective-permute-start.14 = (bf16[256,2048]{1,0:T(8,128)(2,1)}, bf16[256,2048]{1,0:T(8,128)(2,1)}, u32[]{:S(2)}, u32[]{:S(2)}) collective-permute-start(bf16[256,2048]{1,0:T(8,128)(2,1)} %get-tuple-element.10), channel_id=1, source_target_pairs={{0,6},{2,0},{4,2},{6,4},{1,7},{3,1},{5,3},{7,5},{8,14},{10,8},{12,... | collective-permute-start | bytes 3145736 | tf_op jit(solution)/shard_map/ppermute | solution.py:17
  66.0 19.1 %collective-permute-done.13.refs_2_ = bf16[256,2048]{1,0:T(8,128)(2,1)S(1)} collective-permute-done((bf16[256,2048]{1,0:T(8,128)(2,1)}, bf16[256,2048]{1,0:T(8,128)(2,1)S(1)}, u32[]{:S(2)}, u32[]{:S(2)}) %collective-permute-start.13) | collective-permute-done | bytes 1048608 | tf_op jit(solution)/shard_map/ppermute | solution.py:17
  85.0 6.8 %collective-permute-start.15 = (bf16[256,2048]{1,0:T(8,128)(2,1)}, bf16[256,2048]{1,0:T(8,128)(2,1)}, u32[]{:S(2)}, u32[]{:S(2)}) collective-permute-start(bf16[256,2048]{1,0:T(8,128)(2,1)} %get-tuple-element.9), channel_id=1, source_target_pairs={{0,6},{2,0},{4,2},{6,4},{1,7},{3,1},{5,3},{7,5},{8,14},{10,8},{12,... | collective-permute-start | bytes 3145736 | tf_op jit(solution)/shard_map/ppermute | solution.py:17
  91.8 2.3 %collective-permute-start.9 = (bf16[512,512]{1,0:T(8,128)(2,1)}, bf16[512,512]{1,0:T(8,128)(2,1)}, u32[]{:S(2)}, u32[]{:S(2)}) collective-permute-start(bf16[512,512]{1,0:T(8,128)(2,1)} %collective-permute-done.7), channel_id=1, source_target_pairs={{0,224},{32,0},{64,32},{96,64},{128,96},{160,128},{192,160},{224,1... | collective-permute-start | bytes 1572872 | tf_op jit(solution)/shard_map/ppermute | solution.py:17
  95.7 6.6 %all-to-all-start.1 = ((bf16[32,16,128]{2,1,0:T(8,128)(2,1)}), bf16[32,16,128]{2,1,0:T(8,128)(2,1)}, u32[]{:S(2)}, u32[]{:S(2)}) async-start(bf16[32,16,128]{2,1,0:T(8,128)(2,1)} %bitcast.25), calls=%async_computation.1 | async-start | bytes 262144 | tf_op jit(solution)/shard_map/all_to_all | solution.py:147
  103.8 2.6 %collective-permute-done.9 = bf16[512,512]{1,0:T(8,128)(2,1)} collective-permute-done((bf16[512,512]{1,0:T(8,128)(2,1)}, bf16[512,512]{1,0:T(8,128)(2,1)}, u32[]{:S(2)}, u32[]{:S(2)}) %collective-permute-start.9) | collective-permute-done | bytes 524320 | tf_op jit(solution)/shard_map/ppermute | solution.py:17
  106.5 2.4 %broadcast_in_dim.42 = bf16[8,512,512]{2,1,0:T(8,128)(2,1)} broadcast(bf16[]{:T(256)} %constant.147.clone.1), dimensions={} | broadcast | bytes 4194306 | tf_op jit(solution)/shard_map/broadcast_in_dim | solution.py:42
  109.8 1.9 bitcast_dynamic-update-slice_fusion.5
  118.4 1.9 bitcast_dynamic-update-slice_fusion.4
  120.3 1.9 bitcast_dynamic-update-slice_fusion.3
  123.6 1.9 bitcast_dynamic-update-slice_fusion.2
  125.5 1.9 bitcast_dynamic-update-slice_fusion.1
  127.4 1.9 bitcast_dynamic-update-slice_fusion
  129.2 7.6 %collective-permute-done.21.refs_0_ = bf16[256,2048]{1,0:T(8,128)(2,1)S(1)} collective-permute-done((bf16[256,2048]{1,0:T(8,128)(2,1)S(1)}, bf16[256,2048]{1,0:T(8,128)(2,1)S(1)}, u32[]{:S(2)}, u32[]{:S(2)}) %collective-permute-start.21) | collective-permute-done | bytes 1048608 | tf_op jit(solution)/shard_map/ppermute | solution.py:17
  136.8 2.6 %collective-permute-done.22.refs_1_ = bf16[256,2048]{1,0:T(8,128)(2,1)S(1)} collective-permute-done((bf16[256,2048]{1,0:T(8,128)(2,1)}, bf16[256,2048]{1,0:T(8,128)(2,1)S(1)}, u32[]{:S(2)}, u32[]{:S(2)}) %collective-permute-start.22) | collective-permute-done | bytes 1048608 | tf_op jit(solution)/shard_map/ppermute | solution.py:17
  144.6 13.4 %first_slices.1 = (f32[512,2048]{1,0:T(8,128)}, bf16[512,128]{1,0:T(8,128)(2,1)S(1)}) custom-call(s32[6]{0:T(128)S(1)} %stack.36.slot_ref, bf16[8,512,512]{2,1,0:T(8,128)(2,1)} %bitcast_dynamic-update-slice_fusion.7.hid_ref, bf16[8,512,128]{2,1,0:T(8,128)(2,1)S(1)} %bitcast.45, bf16[512,2048]{1,0:T(8,128)(2,1)} %refs_0_.1, bf16[256,2048]{1,0:T(8,128)(2,1)S(1)} %copy-done.3, ...), custom_call_target="tpu_custom_call" | custom-call | flops 6442450944 | bytes 20971520 | tf_op jit(solution)/shard_map/first_slices/pallas_call | solution.py:174
  158.0 11.5 %last_slices.1 = f32[512,256]{1,0:T(8,128)} custom-call(s32[2]{0:T(128)S(1)} %pad_add_fusion.slot_ref, bf16[8,512,512]{2,1,0:T(8,128)(2,1)} %bitcast_dynamic-update-slice_fusion.7.hid_ref, f32[512,2048]{1,0:T(8,128)} %get-tuple-element.8.part_ref, bf16[2048,128]{1,0:T(8,128)(2,1)S(1)} %copy-done.1, s32[512,1]{1,0:T(8,128)S(1)} %copy.13.tgt_ref, ...), custom_call_target="tpu_custom_call" | custom-call | flops 2415919104 | bytes 14680064 | tf_op jit(solution)/shard_map/last_slices/pallas_call | solution.py:188
  169.5 7.9 %all-to-all-start = ((f32[32,16,256]{2,1,0:T(8,128)}), f32[32,16,256]{2,1,0:T(8,128)S(1)}, u32[]{:S(2)}, u32[]{:S(2)}) async-start(f32[32,16,256]{2,1,0:T(8,128)} %bitcast.24), calls=%async_computation | async-start | bytes 1048576 | tf_op jit(solution)/shard_map/all_to_all | solution.py:209
  177.6 18.2 %all-to-all-done.got_ref = f32[32,16,256]{2,1,0:T(8,128)S(1)} async-done(((f32[32,16,256]{2,1,0:T(8,128)}), f32[32,16,256]{2,1,0:T(8,128)S(1)}, u32[]{:S(2)}, u32[]{:S(2)}) %all-to-all-start) | async-done | bytes 524320 | tf_op jit(solution)/shard_map/all_to_all | solution.py:209
  196.6 2.1 merge.1
  198.7 4.7 %all-to-all-start.2 = ((f32[32,16,128]{2,1,0:T(8,128)}), f32[32,16,128]{2,1,0:T(8,128)S(1)}, u32[]{:S(2)}, u32[]{:S(2)}) async-start(f32[32,16,128]{2,1,0:T(8,128)} %merge.1), calls=%async_computation.2 | async-start | bytes 524288 | tf_op jit(solution)/shard_map/all_to_all | solution.py:215
  203.7 12.0 %all-to-all-done.2 = f32[32,16,128]{2,1,0:T(8,128)S(1)} async-done(((f32[32,16,128]{2,1,0:T(8,128)}), f32[32,16,128]{2,1,0:T(8,128)S(1)}, u32[]{:S(2)}, u32[]{:S(2)}) %all-to-all-start.2) | async-done | bytes 262176 | tf_op jit(solution)/shard_map/all_to_all | solution.py:215
  (80 shorter events, 28.8 us)
Async XLA Ops:
  6.5 87.6 %copy-start.8 = (s32[512]{0:T(512)S(1)}, s32[512]{0:T(512)}, u32[]{:S(2)}) copy-start(s32[512]{0:T(512)} %param.10) | copy-start | bytes 6148
  6.5 87.6 %copy-start = (bf16[2048,128]{1,0:T(8,128)(2,1)S(1)}, bf16[2048,128]{1,0:T(8,128)(2,1)}, u32[]{:S(2)}) copy-start(bf16[2048,128]{1,0:T(8,128)(2,1)} %proj_ref.1) | copy-start | bytes 1572868
  6.5 134.3 %all-gather.3.cloned.1.call-start = ((), (), s32[]{:S(2)}) async-start(), calls=%async_computation.3 | async-start | bytes 1179648 | tf_op jit(solution)/shard_map/all_gather | solution.py:150
  6.5 15.9 %collective-permute-start = (bf16[128,512]{1,0:T(8,128)(2,1)}, bf16[128,512]{1,0:T(8,128)(2,1)S(1)}, u32[]{:S(2)}, u32[]{:S(2)}) collective-permute-start(bf16[128,512]{1,0:T(8,128)(2,1)} %param.6), channel_id=1, source_target_pairs={{0,0},{1,32},{2,64},{3,96},{4,128},{5,160},{6,192},{7,224},{8,8},{... | collective-permute-start | bytes 393224 | tf_op jit(solution)/shard_map/ppermute | solution.py:32
  22.4 6.2 %collective-permute-start.1 = (bf16[128,512]{1,0:T(8,128)(2,1)S(1)}, bf16[128,512]{1,0:T(8,128)(2,1)S(1)}, u32[]{:S(2)}, u32[]{:S(2)}) collective-permute-start(bf16[128,512]{1,0:T(8,128)(2,1)S(1)} %collective-permute-done), channel_id=1, source_target_pairs={{0,8},{8,16},{16,24},{24,0},{1,9},{9,17},{17,25},{25,1},{2,10},{10... | collective-permute-start | bytes 393224 | tf_op jit(solution)/shard_map/ppermute | solution.py:17
  23.9 5.0 %collective-permute-start.2 = (bf16[128,512]{1,0:T(8,128)(2,1)S(1)}, bf16[128,512]{1,0:T(8,128)(2,1)S(1)}, u32[]{:S(2)}, u32[]{:S(2)}) collective-permute-start(bf16[128,512]{1,0:T(8,128)(2,1)S(1)} %collective-permute-done), channel_id=1, source_target_pairs={{0,24},{8,0},{16,8},{24,16},{1,25},{9,1},{17,9},{25,17},{2,26},{10... | collective-permute-start | bytes 393224 | tf_op jit(solution)/shard_map/ppermute | solution.py:17
  25.7 6.5 %collective-permute-start.3 = (bf16[128,512]{1,0:T(8,128)(2,1)S(1)}, bf16[128,512]{1,0:T(8,128)(2,1)S(1)}, u32[]{:S(2)}, u32[]{:S(2)}) collective-permute-start(bf16[128,512]{1,0:T(8,128)(2,1)S(1)} %collective-permute-done), channel_id=1, source_target_pairs={{0,16},{8,24},{16,0},{24,8},{1,17},{9,25},{17,1},{25,9},{2,18},{10... | collective-permute-start | bytes 393224 | tf_op jit(solution)/shard_map/ppermute | solution.py:17
  32.2 14.5 %collective-permute-start.4 = (bf16[512,512]{1,0:T(8,128)(2,1)S(1)}, bf16[512,512]{1,0:T(8,128)(2,1)}, u32[]{:S(2)}, u32[]{:S(2)}) collective-permute-start(bf16[512,512]{1,0:T(8,128)(2,1)S(1)} %constant_dynamic-update-slice_fusion), channel_id=1, source_target_pairs={{0,32},{32,64},{64,96},{96,128},{128,160},{160,192},{192,224},{224... | collective-permute-start | bytes 1572872 | tf_op jit(solution)/shard_map/ppermute | solution.py:17
  35.8 26.3 %collective-permute-start.12 = (bf16[256,2048]{1,0:T(8,128)(2,1)}, bf16[256,2048]{1,0:T(8,128)(2,1)S(1)}, u32[]{:S(2)}, u32[]{:S(2)}) collective-permute-start(bf16[256,2048]{1,0:T(8,128)(2,1)} %get-tuple-element.10), channel_id=1, source_target_pairs={{0,2},{2,4},{4,6},{6,0},{1,3},{3,5},{5,7},{7,1},{8,10},{10,12},{12... | collective-permute-start | bytes 3145736 | tf_op jit(solution)/shard_map/ppermute | solution.py:17
  36.6 48.4 %collective-permute-start.13 = (bf16[256,2048]{1,0:T(8,128)(2,1)}, bf16[256,2048]{1,0:T(8,128)(2,1)S(1)}, u32[]{:S(2)}, u32[]{:S(2)}) collective-permute-start(bf16[256,2048]{1,0:T(8,128)(2,1)} %get-tuple-element.9), channel_id=1, source_target_pairs={{0,2},{2,4},{4,6},{6,0},{1,3},{3,5},{5,7},{7,1},{8,10},{10,12},{12... | collective-permute-start | bytes 3145736 | tf_op jit(solution)/shard_map/ppermute | solution.py:17
  41.2 13.2 %collective-permute-start.5 = (bf16[512,512]{1,0:T(8,128)(2,1)S(1)}, bf16[512,512]{1,0:T(8,128)(2,1)}, u32[]{:S(2)}, u32[]{:S(2)}) collective-permute-start(bf16[512,512]{1,0:T(8,128)(2,1)S(1)} %constant_dynamic-update-slice_fusion), channel_id=1, source_target_pairs={{0,224},{32,0},{64,32},{96,64},{128,96},{160,128},{192,160},{224,1... | collective-permute-start | bytes 1572872 | tf_op jit(solution)/shard_map/ppermute | solution.py:17
  46.6 13.0 %collective-permute-start.6 = (bf16[512,512]{1,0:T(8,128)(2,1)}, bf16[512,512]{1,0:T(8,128)(2,1)}, u32[]{:S(2)}, u32[]{:S(2)}) collective-permute-start(bf16[512,512]{1,0:T(8,128)(2,1)} %collective-permute-done.4), channel_id=1, source_target_pairs={{0,32},{32,64},{64,96},{96,128},{128,160},{160,192},{192,224},{224... | collective-permute-start | bytes 1572872 | tf_op jit(solution)/shard_map/ppermute | solution.py:17
  54.4 37.5 %collective-permute-start.7 = (bf16[512,512]{1,0:T(8,128)(2,1)}, bf16[512,512]{1,0:T(8,128)(2,1)}, u32[]{:S(2)}, u32[]{:S(2)}) collective-permute-start(bf16[512,512]{1,0:T(8,128)(2,1)} %collective-permute-done.5), channel_id=1, source_target_pairs={{0,224},{32,0},{64,32},{96,64},{128,96},{160,128},{192,160},{224,1... | collective-permute-start | bytes 1572872 | tf_op jit(solution)/shard_map/ppermute | solution.py:17
  57.9 65.1 %collective-permute-start.16 = (bf16[512,2048]{1,0:T(8,128)(2,1)}, bf16[512,2048]{1,0:T(8,128)(2,1)}, u32[]{:S(2)}, u32[]{:S(2)}) collective-permute-start(bf16[512,2048]{1,0:T(8,128)(2,1)} %refs_0_.1), channel_id=1, source_target_pairs={{0,1},{1,0},{2,3},{3,2},{4,5},{5,4},{6,7},{7,6},{8,9},{9,8},{10,11... | collective-permute-start | bytes 6291464 | tf_op jit(solution)/shard_map/ppermute | solution.py:17
  59.6 42.7 %collective-permute-start.8 = (bf16[512,512]{1,0:T(8,128)(2,1)}, bf16[512,512]{1,0:T(8,128)(2,1)}, u32[]{:S(2)}, u32[]{:S(2)}) collective-permute-start(bf16[512,512]{1,0:T(8,128)(2,1)} %collective-permute-done.6), channel_id=1, source_target_pairs={{0,32},{32,64},{64,96},{96,128},{128,160},{160,192},{192,224},{224... | collective-permute-start | bytes 1572872 | tf_op jit(solution)/shard_map/ppermute | solution.py:17
  62.2 50.5 %copy-start.2 = (bf16[256,2048]{1,0:T(8,128)(2,1)}, bf16[256,2048]{1,0:T(8,128)(2,1)S(1)}, u32[]{:S(2)}) copy-start(bf16[256,2048]{1,0:T(8,128)(2,1)S(1)} %collective-permute-done.12.refs_1_) | copy-start | bytes 3145732
  62.2 50.5 %collective-permute-start.14 = (bf16[256,2048]{1,0:T(8,128)(2,1)}, bf16[256,2048]{1,0:T(8,128)(2,1)}, u32[]{:S(2)}, u32[]{:S(2)}) collective-permute-start(bf16[256,2048]{1,0:T(8,128)(2,1)} %get-tuple-element.10), channel_id=1, source_target_pairs={{0,6},{2,0},{4,2},{6,4},{1,7},{3,1},{5,3},{7,5},{8,14},{10,8},{12,... | collective-permute-start | bytes 3145736 | tf_op jit(solution)/shard_map/ppermute | solution.py:17
  85.0 30.2 %collective-permute-start.15 = (bf16[256,2048]{1,0:T(8,128)(2,1)}, bf16[256,2048]{1,0:T(8,128)(2,1)}, u32[]{:S(2)}, u32[]{:S(2)}) collective-permute-start(bf16[256,2048]{1,0:T(8,128)(2,1)} %get-tuple-element.9), channel_id=1, source_target_pairs={{0,6},{2,0},{4,2},{6,4},{1,7},{3,1},{5,3},{7,5},{8,14},{10,8},{12,... | collective-permute-start | bytes 3145736 | tf_op jit(solution)/shard_map/ppermute | solution.py:17
  91.8 14.6 %collective-permute-start.9 = (bf16[512,512]{1,0:T(8,128)(2,1)}, bf16[512,512]{1,0:T(8,128)(2,1)}, u32[]{:S(2)}, u32[]{:S(2)}) collective-permute-start(bf16[512,512]{1,0:T(8,128)(2,1)} %collective-permute-done.7), channel_id=1, source_target_pairs={{0,224},{32,0},{64,32},{96,64},{128,96},{160,128},{192,160},{224,1... | collective-permute-start | bytes 1572872 | tf_op jit(solution)/shard_map/ppermute | solution.py:17
  95.7 73.9 %all-to-all-start.1 = ((bf16[32,16,128]{2,1,0:T(8,128)(2,1)}), bf16[32,16,128]{2,1,0:T(8,128)(2,1)}, u32[]{:S(2)}, u32[]{:S(2)}) async-start(bf16[32,16,128]{2,1,0:T(8,128)(2,1)} %bitcast.25), calls=%async_computation.1 | async-start | bytes 262144 | tf_op jit(solution)/shard_map/all_to_all | solution.py:147
  102.3 21.2 %collective-permute-start.17 = (bf16[256,2048]{1,0:T(8,128)(2,1)S(1)}, bf16[256,2048]{1,0:T(8,128)(2,1)}, u32[]{:S(2)}, u32[]{:S(2)}) collective-permute-start(bf16[256,2048]{1,0:T(8,128)(2,1)S(1)} %collective-permute-done.12.refs_1_), channel_id=1, source_target_pairs={{0,1},{1,0},{2,3},{3,2},{4,5},{5,4},{6,7},{7,6},{8,9},{9,8},{10,11... | collective-permute-start | bytes 3145736 | tf_op jit(solution)/shard_map/ppermute | solution.py:17
  106.4 10.2 %collective-permute-start.10 = (bf16[256,512]{1,0:T(8,128)(2,1)S(1)}, bf16[256,512]{1,0:T(8,128)(2,1)S(1)}, u32[]{:S(2)}, u32[]{:S(2)}) collective-permute-start(bf16[256,512]{1,0:T(8,128)(2,1)S(1)} %slice.16), channel_id=1, source_target_pairs={{0,32},{32,64},{64,96},{96,128},{128,160},{160,192},{192,224},{224... | collective-permute-start | bytes 786440 | tf_op jit(solution)/shard_map/ppermute | solution.py:17
  112.6 24.2 %collective-permute-start.21 = (bf16[256,2048]{1,0:T(8,128)(2,1)S(1)}, bf16[256,2048]{1,0:T(8,128)(2,1)S(1)}, u32[]{:S(2)}, u32[]{:S(2)}) collective-permute-start(bf16[256,2048]{1,0:T(8,128)(2,1)S(1)} %collective-permute-done.12.refs_1_), channel_id=1, source_target_pairs={{0,2},{2,4},{4,6},{6,0},{1,3},{3,5},{5,7},{7,1},{8,10},{10,12},{12... | collective-permute-start | bytes 3145736 | tf_op jit(solution)/shard_map/ppermute | solution.py:17
  115.3 24.1 %collective-permute-start.22 = (bf16[256,2048]{1,0:T(8,128)(2,1)}, bf16[256,2048]{1,0:T(8,128)(2,1)S(1)}, u32[]{:S(2)}, u32[]{:S(2)}) collective-permute-start(bf16[256,2048]{1,0:T(8,128)(2,1)} %collective-permute-done.15.refs_4_), channel_id=1, source_target_pairs={{0,6},{2,0},{4,2},{6,4},{1,7},{3,1},{5,3},{7,5},{8,14},{10,8},{12,... | collective-permute-start | bytes 3145736 | tf_op jit(solution)/shard_map/ppermute | solution.py:17
  116.6 6.4 %collective-permute-start.11 = (bf16[256,512]{1,0:T(8,128)(2,1)S(1)}, bf16[256,512]{1,0:T(8,128)(2,1)S(1)}, u32[]{:S(2)}, u32[]{:S(2)}) collective-permute-start(bf16[256,512]{1,0:T(8,128)(2,1)S(1)} %slice.17), channel_id=1, source_target_pairs={{0,224},{32,0},{64,32},{96,64},{128,96},{160,128},{192,160},{224,1... | collective-permute-start | bytes 786440 | tf_op jit(solution)/shard_map/ppermute | solution.py:17
  123.0 17.9 %collective-permute-start.20 = (bf16[256,2048]{1,0:T(8,128)(2,1)}, bf16[256,2048]{1,0:T(8,128)(2,1)}, u32[]{:S(2)}, u32[]{:S(2)}) collective-permute-start(bf16[256,2048]{1,0:T(8,128)(2,1)} %collective-permute-done.15.refs_4_), channel_id=1, source_target_pairs={{0,1},{1,0},{2,3},{3,2},{4,5},{5,4},{6,7},{7,6},{8,9},{9,8},{10,11... | collective-permute-start | bytes 3145736 | tf_op jit(solution)/shard_map/ppermute | solution.py:17
  123.0 17.8 %collective-permute-start.18 = (bf16[256,2048]{1,0:T(8,128)(2,1)}, bf16[256,2048]{1,0:T(8,128)(2,1)}, u32[]{:S(2)}, u32[]{:S(2)}) collective-permute-start(bf16[256,2048]{1,0:T(8,128)(2,1)} %copy-done.4), channel_id=1, source_target_pairs={{0,1},{1,0},{2,3},{3,2},{4,5},{5,4},{6,7},{7,6},{8,9},{9,8},{10,11... | collective-permute-start | bytes 3145736 | tf_op jit(solution)/shard_map/ppermute | solution.py:17
  123.5 17.3 %collective-permute-start.19 = (bf16[256,2048]{1,0:T(8,128)(2,1)}, bf16[256,2048]{1,0:T(8,128)(2,1)}, u32[]{:S(2)}, u32[]{:S(2)}) collective-permute-start(bf16[256,2048]{1,0:T(8,128)(2,1)} %collective-permute-done.14.refs_3_), channel_id=1, source_target_pairs={{0,1},{1,0},{2,3},{3,2},{4,5},{5,4},{6,7},{7,6},{8,9},{9,8},{10,11... | collective-permute-start | bytes 3145736 | tf_op jit(solution)/shard_map/ppermute | solution.py:17
  136.8 21.2 %collective-permute-start.23 = (bf16[256,2048]{1,0:T(8,128)(2,1)S(1)}, bf16[256,2048]{1,0:T(8,128)(2,1)S(1)}, u32[]{:S(2)}, u32[]{:S(2)}) collective-permute-start(bf16[256,2048]{1,0:T(8,128)(2,1)S(1)} %collective-permute-done.21.refs_0_), channel_id=1, source_target_pairs={{0,1},{1,0},{2,3},{3,2},{4,5},{5,4},{6,7},{7,6},{8,9},{9,8},{10,11... | collective-permute-start | bytes 3145736 | tf_op jit(solution)/shard_map/ppermute | solution.py:17
  139.4 18.6 %collective-permute-start.24 = (bf16[256,2048]{1,0:T(8,128)(2,1)S(1)}, bf16[256,2048]{1,0:T(8,128)(2,1)}, u32[]{:S(2)}, u32[]{:S(2)}) collective-permute-start(bf16[256,2048]{1,0:T(8,128)(2,1)S(1)} %collective-permute-done.22.refs_1_), channel_id=1, source_target_pairs={{0,1},{1,0},{2,3},{3,2},{4,5},{5,4},{6,7},{7,6},{8,9},{9,8},{10,11... | collective-permute-start | bytes 3145736 | tf_op jit(solution)/shard_map/ppermute | solution.py:17
  169.5 26.3 %all-to-all-start = ((f32[32,16,256]{2,1,0:T(8,128)}), f32[32,16,256]{2,1,0:T(8,128)S(1)}, u32[]{:S(2)}, u32[]{:S(2)}) async-start(f32[32,16,256]{2,1,0:T(8,128)} %bitcast.24), calls=%async_computation | async-start | bytes 1048576 | tf_op jit(solution)/shard_map/all_to_all | solution.py:209
  198.7 17.0 %all-to-all-start.2 = ((f32[32,16,128]{2,1,0:T(8,128)}), f32[32,16,128]{2,1,0:T(8,128)S(1)}, u32[]{:S(2)}, u32[]{:S(2)}) async-start(f32[32,16,128]{2,1,0:T(8,128)} %merge.1), calls=%async_computation.2 | async-start | bytes 524288 | tf_op jit(solution)/shard_map/all_to_all | solution.py:215
  (7 other events, 64.9 us)
Sparse Core Ops, SparseCore 0:
  59.8 28.6 all-gather.2

commit v2 on v1

v2 whole, which is shorter than its diff:
```python
import functools

import jax
import jax.numpy as jnp
from jax import lax
from jax.experimental import pallas as pl
from jax.experimental.pallas import tpu as pltpu
from jax.sharding import Mesh, PartitionSpec as P

TILE = 512
FA = 1 << 20
FB = 1 << 20
SLICE = 1 << 36
F32 = jnp.float32
BF16 = jnp.bfloat16


def shift(x, axis, by):
    n = lax.axis_size(axis)
    return lax.ppermute(x, axis, [(i, (i + by) % n) for i in range(n)])


def swap(x):
    return shift(x, "c", 1)


def exchange_corners(x):
    pairs = []
    for z in range(8):
        for xx in range(4):
            for v in range(8):
                src = (z * 4 + xx) * 8 + v
                dst = (v * 4 + xx) * 8 + z
                pairs.append((src, dst))
    return lax.ppermute(x, ("z", "x", "y", "c"), pairs)


def along_x(block):
    x = lax.axis_index("x")
    out = jnp.zeros((512, 512), BF16)
    for by in (0, 1, 3, 2):
        got = block if by == 0 else shift(block, "x", by)
        out = lax.dynamic_update_slice(out, got, (((x - by) % 4) * 128, 0))
    return out


def halves_kernel(up_ref, down_ref, early_ref, a_ref, b_ref):
    a_ref[...] = up_ref[...]
    b_ref[...] = down_ref[...]


def halves(up, down, early):
    half = jax.ShapeDtypeStruct((256, 2048), BF16)
    block = (128, 2048)
    return pl.pallas_call(
        halves_kernel,
        out_shape=(half, half),
        grid=(2,),
        in_specs=[
            pl.BlockSpec(block, lambda i: (i, 0)),
            pl.BlockSpec(block, lambda i: (i + 2, 0)),
            pl.BlockSpec(memory_space=pl.ANY),
        ],
        out_specs=(pl.BlockSpec(block, lambda i: (i, 0)), pl.BlockSpec(block, lambda i: (i, 0))),
        cost_estimate=pl.CostEstimate(flops=SLICE, bytes_accessed=4 << 20, transcendentals=0),
        name="halves",
    )(up, down, early)


def dots(hid_ref, slot_ref, pieces, refs, acc):
    for ref, (place, low, rows) in zip(refs, pieces):
        part = jnp.dot(
            hid_ref[slot_ref[place], :, low : low + rows], ref[...], preferred_element_type=F32
        )
        acc = part if acc is None else acc + part
    return acc


def first_kernel(pieces, slot_ref, hid_ref, *refs):
    heads, part_ref = refs[: len(pieces)], refs[len(pieces)]
    part_ref[...] = dots(hid_ref, slot_ref, pieces, heads, None)


def last_kernel(pieces, slot_ref, hid_ref, part_ref, proj_ref, tgt_ref, rows_ref, *refs):
    heads, (out_ref, max_ref, rest_ref, hit_ref, sum_ref) = refs[: len(pieces)], refs[len(pieces) :]
    step = pl.program_id(0)

    @pl.when(step == 0)
    def _():
        max_ref[...] = jnp.full_like(max_ref, -jnp.inf)
        rest_ref[...] = jnp.zeros_like(rest_ref)
        hit_ref[...] = jnp.zeros_like(hit_ref)
        sum_ref[...] = jnp.zeros_like(sum_ref)

    logits = dots(hid_ref, slot_ref, pieces, heads, part_ref[...])
    old = max_ref[...]
    new = jnp.maximum(old, jnp.max(logits, axis=1, keepdims=True))
    scale = jnp.exp(old - new)
    shifted = jnp.exp(logits - new)
    columns = lax.broadcasted_iota(jnp.int32, logits.shape, 1) + step * TILE
    at_target = columns == tgt_ref[...]
    rest = jnp.where(at_target, 0.0, shifted)
    hit = jnp.where(at_target, shifted, 0.0)
    max_ref[...] = new
    rest_ref[...] = rest_ref[...] * scale + jnp.sum(rest, axis=1, keepdims=True)
    hit_ref[...] = hit_ref[...] * scale + jnp.sum(hit, axis=1, keepdims=True)
    sum_ref[...] = sum_ref[...] * scale + jnp.dot(
        rest.astype(BF16), proj_ref[...], preferred_element_type=F32
    )

    @pl.when(step == pl.num_programs(0) - 1)
    def _():
        out_ref[:, :128] = sum_ref[...].astype(BF16)
        lane = lax.broadcasted_iota(jnp.int32, (512, 128), 1)
        stats = jnp.where(lane < 3, max_ref[...], jnp.where(lane < 6, rest_ref[...], hit_ref[...]))
        high = stats.astype(BF16).astype(F32)
        middle = (stats - high).astype(BF16).astype(F32)
        low = stats - high - middle
        term = lane % 3
        out_ref[:, 256:] = rows_ref[...]
        out_ref[:, 128:256] = jnp.where(term == 0, high, jnp.where(term == 1, middle, low)).astype(BF16)


def merge_kernel(got_ref, out_ref):
    terms = got_ref[:, :, 128:256].astype(F32)
    top, rest, hit = (
        terms[:, :, i : i + 1] + terms[:, :, i + 1 : i + 2] + terms[:, :, i + 2 : i + 3]
        for i in (0, 3, 6)
    )
    weight = jnp.exp(top - jnp.max(top, axis=0, keepdims=True))
    rest = jnp.sum(weight * rest, axis=0)
    hit = jnp.sum(weight * hit, axis=0)
    total = jnp.sum(weight * got_ref[:, :, :128].astype(F32), axis=0)
    row = jnp.sum(got_ref[:, :, 256:].astype(F32), axis=0)
    merged = ((total - rest * row) / (rest + hit)).astype(BF16)
    out_ref[...] = jnp.broadcast_to(merged[None], out_ref.shape)


PARAMS = dict(dimension_semantics=("arbitrary",), vmem_limit_bytes=48 << 20)


def head_spec(ref):
    return pl.BlockSpec((ref.shape[0], TILE), lambda i, s: (0, i))


def whole(shape):
    return pl.BlockSpec(shape, lambda i, s: (0,) * len(shape))


def local(hidden_states, head, proj_in, proj_out, targets, lengths):
    z, x, y, c = (lax.axis_index(a) for a in ("z", "x", "y", "c"))
    me = z * 4 + x

    up, down = shift(head, "y", 1), shift(head, "y", -1)
    pin = lax.all_gather(exchange_corners(proj_in), "z", axis=0, tiled=False)
    mine = along_x(exchange_corners(hidden_states))
    hid = lax.all_gather(mine, "z", axis=0, tiled=False)
    far_a, far_b = halves(up, down, mine)
    far_a, far_b = shift(far_a, "y", 1), shift(far_b, "y", -1)

    local_target = targets[:, None] - me * 2048
    onehot = (local_target == jnp.arange(2048, dtype=jnp.int32)[None, :]).astype(BF16)
    rows = jnp.dot(onehot, proj_out, preferred_element_type=F32).astype(BF16)

    def slot(dy, dc):
        return ((y + dy) % 4) * 2 + (c + dc) % 2

    near = [(head, 0, 0, 512), (up, 1, 0, 512), (down, 2, 0, 512)]
    far = [(far_a, 0, 0, 256), (far_b, 0, 256, 256)]

    def both(items, count):
        refs = [i[0] for i in items] + [swap(i[0]) for i in items]
        pieces = [i[1:] for i in items] + [(i[1] + count, i[2], i[3]) for i in items]
        return refs, pieces

    near_refs, near_pieces = both(near, 3)
    far_refs, far_pieces = both(far, 1)
    near_slots = jnp.stack([slot(dy, dc) for dc in (0, 1) for dy in (0, -1, 1)]).astype(jnp.int32)
    far_slots = jnp.stack([slot(2, dc) for dc in (0, 1)]).astype(jnp.int32)

    part = pl.pallas_call(
        functools.partial(first_kernel, near_pieces),
        out_shape=jax.ShapeDtypeStruct((512, 2048), F32),
        grid_spec=pltpu.PrefetchScalarGridSpec(
            num_scalar_prefetch=1,
            grid=(2048 // TILE,),
            in_specs=[whole((8, 512, 512))] + [head_spec(r) for r in near_refs],
            out_specs=pl.BlockSpec((512, TILE), lambda i, s: (0, i)),
        ),
        compiler_params=pltpu.CompilerParams(**PARAMS),
        cost_estimate=pl.CostEstimate(flops=FA, bytes_accessed=1 << 20, transcendentals=0),
        name="first_slices",
    )(near_slots, hid, *near_refs)

    out = pl.pallas_call(
        functools.partial(last_kernel, far_pieces),
        out_shape=jax.ShapeDtypeStruct((512, 384), BF16),
        grid_spec=pltpu.PrefetchScalarGridSpec(
            num_scalar_prefetch=1,
            grid=(2048 // TILE,),
            in_specs=[
                whole((8, 512, 512)),
                pl.BlockSpec((512, TILE), lambda i, s: (0, i)),
                pl.BlockSpec((TILE, 128), lambda i, s: (i, 0)),
                whole((512, 1)),
                whole((512, 128)),
            ]
            + [head_spec(r) for r in far_refs],
            out_specs=whole((512, 384)),
            scratch_shapes=[pltpu.VMEM((512, 1), F32)] * 3 + [pltpu.VMEM((512, 128), F32)],
        ),
        compiler_params=pltpu.CompilerParams(**PARAMS),
        cost_estimate=pl.CostEstimate(flops=FB, bytes_accessed=1 << 20, transcendentals=0),
        name="last_slices",
    )(far_slots, hid, part, proj_out, local_target, rows, *far_refs)

    got = lax.all_to_all(out, ("z", "x"), 0, 0, tiled=True).reshape(32, 16, 384)
    merged = pl.pallas_call(
        merge_kernel,
        out_shape=jax.ShapeDtypeStruct((32, 16, 128), BF16),
        name="merge",
    )(got)
    out_proj = lax.all_to_all(merged, ("z", "x"), 0, 0, tiled=True).reshape(512, 128).astype(F32)

    seq_lengths = lengths[0]
    ends = jnp.cumsum(seq_lengths)
    starts = ends - seq_lengths
    positions = jnp.arange(512, dtype=jnp.int32)
    member = (
        (positions[:, None] >= starts[None, :]) & (positions[:, None] < ends[None, :])
    ).astype(F32)
    membership = member / seq_lengths.astype(F32)[None, :]
    in_proj = sum(jnp.dot(hid[d], pin[d], preferred_element_type=F32) for d in range(8)).astype(BF16)
    in_slice = lax.dynamic_slice_in_dim(in_proj, me * 4, 4, 1)
    expanded = membership[:, :, None] * in_slice.astype(F32)[:, None, :]
    return jnp.einsum("ter,tc->erc", expanded, out_proj, precision=lax.Precision.HIGHEST)


def solution(mesh):
    fine = Mesh(mesh.devices.reshape(8, 4, 4, 2), ("z", "x", "y", "c"))
    tok, voc = ("z", "x"), ("y", "c")
    placed = (P(tok, voc), P(voc, tok), P(voc, None), P(tok, None), P(voc), P(voc, None))
    return jax.shard_map(
        local, mesh=fine, in_specs=placed, out_specs=P(voc, tok, None), check_vma=False
    )
```

time: 224 us -> 176 us (0.79)
  starting transfers between devices: 59.3 us -> 34.9 us
  local copies, waits for them, and re-layouts: 26.6 us -> 2.55 us
  waiting for transfers between devices: 94.6 us -> 81.5 us
  matrix products: 1.76 us -> 13 us
    ppermute x24 -> x12, starting transfers between devices: 34.9 us -> 10.2 us  [shift(): return lax.ppermute(x, axis, [(i, (i + by) % n) for i in range(n)])]
    dynamic_update_slice x13 -> x4, local copies, waits for them, and re-layouts: 13.7 us -> 0.06 us  [along_x(): out = lax.dynamic_update_slice(out, got, ((x - by) % 4 * 128, 0))]
    all_to_all x2 -> x1, waiting for transfers between devices: 18.2 us -> 6.32 us  [local(): got = lax.all_to_all(out, ('z', 'x'), 0, 0, tiled=True).reshape(32, 16, 384)]
    dot_general x0 -> x8, matrix products: none -> 11 us  [local(): jnp.dot(hid[d], pin[d], preferred_element_type=F32)]
    slice x3 -> x0, local copies, waits for them, and re-layouts: 5.05 us -> none  [the longest x1 3.11 us: local(): top, bottom = (head[:256], head[256:])]
    all_to_all x1, waiting for transfers between devices: 12 us -> 9.13 us  [local(): lax.all_to_all(merged, ('z', 'x'), 0, 0, tiled=True).reshape(512, 128)]
    unnamed x20 -> x16, local copies, waits for them, and re-layouts: 4.49 us -> 1.61 us
    ppermute x1 -> x2, starting transfers between devices: 5.18 us -> 8.02 us  [exchange_corners(): return lax.ppermute(x, ('z', 'x', 'y', 'c'), pairs)]
  transfers between devices with their start and end apart: 29 -> 18, of which waited for: 16 -> 8; matrix products, arithmetic and copies ran while one was open for 10% -> 8% of each run, Pallas kernels for 11% -> 15%
where the time goes in v2:
time: 176 us; the launch traced here: 175 us
  waiting for transfers between devices  81.5 us (46%)
  starting transfers between devices  34.9 us (20%)
  Pallas kernels  28.6 us (16%)
  between operations  13.7 us (8%)
  matrix products  13 us (7%)
  local copies, waits for them, and re-layouts  2.55 us (1%)
    ppermute x12, waiting for transfers between devices, shift(): return lax.ppermute(x, axis, [(i, (i + by) % n) for i in range(n)])  56.4 us
    all_to_all x1, starting transfers between devices, local(): got = lax.all_to_all(out, ('z', 'x'), 0, 0, tiled=True).reshape(32, 16, 384)  12.4 us
    pallas_call x1, Pallas kernels, local(): pl.pallas_call(functools.partial(first_kernel, near_pieces), out_shape=ja...  12.3 us
    pallas_call x1, Pallas kernels, local(): pl.pallas_call(functools.partial(last_kernel, far_pieces), out_shape=jax....  11.6 us
    dot_general x8, matrix products, local(): jnp.dot(hid[d], pin[d], preferred_element_type=F32)  11 us
    ppermute x12, starting transfers between devices, shift(): return lax.ppermute(x, axis, [(i, (i + by) % n) for i in range(n)])  10.2 us
    ppermute x2, waiting for transfers between devices, exchange_corners(): return lax.ppermute(x, ('z', 'x', 'y', 'c'), pairs)  9.57 us
    all_to_all x1, waiting for transfers between devices, local(): lax.all_to_all(merged, ('z', 'x'), 0, 0, tiled=True).reshape(512, 128)  9.13 us
  transfers between devices with their start and end apart: 18, of which 8 were waited for; matrix products, arithmetic and copies ran while one was open for 8% of the time, Pallas kernels for 15%

profile of v2, /device:TPU:8, one launch (start us, length us, event | category | flops | bytes accessed | tf_op | source)
XLA Modules:
  0.0 175.2 jit_solution(13144411261114397825)
XLA Ops:
  6.5 1.6 collective-permute-start.5
  8.7 6.1 %collective-permute-start = (bf16[128,512]{1,0:T(8,128)(2,1)}, bf16[128,512]{1,0:T(8,128)(2,1)S(1)}, u32[]{:S(2)}, u32[]{:S(2)}) collective-permute-start(bf16[128,512]{1,0:T(8,128)(2,1)} %param.6), channel_id=1, source_target_pairs={{0,0},{1,32},{2,64},{3,96},{4,128},{5,160},{6,192},{7,224},{8,8},{... | collective-permute-start | bytes 393224 | tf_op jit(solution)/shard_map/ppermute | solution.py:35
  14.8 9.6 %collective-permute-done = bf16[128,512]{1,0:T(8,128)(2,1)S(1)} collective-permute-done((bf16[128,512]{1,0:T(8,128)(2,1)}, bf16[128,512]{1,0:T(8,128)(2,1)S(1)}, u32[]{:S(2)}, u32[]{:S(2)}) %collective-permute-start) | collective-permute-done | bytes 131104 | tf_op jit(solution)/shard_map/ppermute | solution.py:35
  24.4 1.5 collective-permute-start.1
  25.9 1.7 collective-permute-start.2
  27.6 1.8 %collective-permute-start.3 = (bf16[128,512]{1,0:T(8,128)(2,1)S(1)}, bf16[128,512]{1,0:T(8,128)(2,1)S(1)}, u32[]{:S(2)}, u32[]{:S(2)}) collective-permute-start(bf16[128,512]{1,0:T(8,128)(2,1)S(1)} %collective-permute-done), channel_id=1, source_target_pairs={{0,16},{8,24},{16,0},{24,8},{1,17},{9,25},{17,1},{25,9},{2,18},{10... | collective-permute-start | bytes 393224 | tf_op jit(solution)/shard_map/ppermute | solution.py:20
  29.5 2.1 %collective-permute-done.1 = bf16[128,512]{1,0:T(8,128)(2,1)S(1)} collective-permute-done((bf16[128,512]{1,0:T(8,128)(2,1)S(1)}, bf16[128,512]{1,0:T(8,128)(2,1)S(1)}, u32[]{:S(2)}, u32[]{:S(2)}) %collective-permute-start.1) | collective-permute-done | bytes 131104 | tf_op jit(solution)/shard_map/ppermute | solution.py:20
  31.7 2.4 %collective-permute-done.3 = bf16[128,512]{1,0:T(8,128)(2,1)S(1)} collective-permute-done((bf16[128,512]{1,0:T(8,128)(2,1)S(1)}, bf16[128,512]{1,0:T(8,128)(2,1)S(1)}, u32[]{:S(2)}, u32[]{:S(2)}) %collective-permute-start.3) | collective-permute-done | bytes 131104 | tf_op jit(solution)/shard_map/ppermute | solution.py:20
  34.1 0.8 copy-done.2
  35.1 1.9 %collective-permute-start.4 = (bf16[512,128]{1,0:T(8,128)(2,1)}, bf16[512,128]{1,0:T(8,128)(2,1)S(1)}, u32[]{:S(2)}, u32[]{:S(2)}) collective-permute-start(bf16[512,128]{1,0:T(8,128)(2,1)} %param.8), channel_id=1, source_target_pairs={{0,0},{1,32},{2,64},{3,96},{4,128},{5,160},{6,192},{7,224},{8,8},{... | collective-permute-start | bytes 393224 | tf_op jit(solution)/shard_map/ppermute | solution.py:35
  37.1 28.4 %collective-permute-done.5.refs_1_.up_ref = bf16[512,2048]{1,0:T(8,128)(2,1)} collective-permute-done((bf16[512,2048]{1,0:T(8,128)(2,1)}, bf16[512,2048]{1,0:T(8,128)(2,1)}, u32[]{:S(2)}, u32[]{:S(2)}) %collective-permute-start.5) | collective-permute-done | bytes 2097184 | tf_op jit(solution)/shard_map/ppermute | solution.py:20
  66.0 2.6 %halves.1 = (bf16[256,2048]{1,0:T(8,128)(2,1)}, bf16[256,2048]{1,0:T(8,128)(2,1)}) custom-call(bf16[512,2048]{1,0:T(8,128)(2,1)} %collective-permute-done.5.refs_1_.up_ref, bf16[512,2048]{1,0:T(8,128)(2,1)} %collective-permute-done.6.refs_2_.down_ref, bf16[512,512]{1,0:T(8,128)(2,1)} %copy-done.2), custom_call_target="tpu_custom_call" | custom-call | flops 68719476736 | bytes 4194304 | tf_op jit(solution)/shard_map/halves/pallas_call | solution.py:55
  68.6 2.0 %collective-permute-start.11 = (bf16[256,2048]{1,0:T(8,128)(2,1)}, bf16[256,2048]{1,0:T(8,128)(2,1)}, u32[]{:S(2)}, u32[]{:S(2)}) collective-permute-start(bf16[256,2048]{1,0:T(8,128)(2,1)} %get-tuple-element.8), channel_id=1, source_target_pairs={{0,6},{2,0},{4,2},{6,4},{1,7},{3,1},{5,3},{7,5},{8,14},{10,8},{12,... | collective-permute-start | bytes 3145736 | tf_op jit(solution)/shard_map/ppermute | solution.py:20
  70.6 23.2 %collective-permute-done.10.refs_0_ = bf16[256,2048]{1,0:T(8,128)(2,1)S(1)} collective-permute-done((bf16[256,2048]{1,0:T(8,128)(2,1)}, bf16[256,2048]{1,0:T(8,128)(2,1)S(1)}, u32[]{:S(2)}, u32[]{:S(2)}) %collective-permute-start.10) | collective-permute-done | bytes 1048608 | tf_op jit(solution)/shard_map/ppermute | solution.py:20
  94.9 0.7 convert_divide_fusion
  95.6 1.9 %fusion.3.rows_ref = bf16[512,128]{1,0:T(8,128)(2,1)S(1)} fusion(bf16[2048,128]{1,0:T(8,128)(2,1)} %proj_ref.1, s32[512]{0:T(512)S(1)} %broadcast_subtract_fusion), kind=kOutput, calls=%fused_computation.5 | convolution fusion | flops 269549568 | bytes 657408 | tf_op jit(solution)/shard_map/dot_general | solution.py:163
  97.6 12.3 %first_slices.1.part_ref = f32[512,2048]{1,0:T(8,128)} custom-call(s32[6]{0:T(128)S(1)} %stack.39.slot_ref, bf16[8,512,512]{2,1,0:T(8,128)(2,1)} %bitcast.26, bf16[512,2048]{1,0:T(8,128)(2,1)S(1)} %copy-done, bf16[512,2048]{1,0:T(8,128)(2,1)} %collective-permute-done.5.refs_1_.up_ref, bf16[512,2048]{1,0:T(8,128)(2,1)} %collective-permute-done.6.refs_2_.down_ref, ...), custom_call_target="tpu_custom_call" | custom-call | flops 1048576 | bytes 1048576 | tf_op jit(solution)/shard_map/first_slices/pallas_call | solution.py:181
  109.9 11.6 %last_slices.1 = bf16[512,384]{1,0:T(8,128)(2,1)} custom-call(s32[2]{0:T(128)S(1)} %pad_add_fusion.slot_ref, bf16[8,512,512]{2,1,0:T(8,128)(2,1)} %bitcast.27, f32[512,2048]{1,0:T(8,128)} %first_slices.1.part_ref, bf16[2048,128]{1,0:T(8,128)(2,1)S(1)} %copy-done.1, s32[512,1]{1,0:T(8,128)S(1)} %copy.8.tgt_ref, bf16[512,128]{1,0:T(8,128)(2,1)S(1)} %fusion.3.rows_ref, ...), custom_call_target="tpu_custom_call" | custom-call | flops 1048576 | bytes 1048576 | tf_op jit(solution)/shard_map/last_slices/pallas_call | solution.py:195
  121.5 12.4 %all-to-all-start = ((bf16[32,16,384]{2,1,0:T(8,128)(2,1)}), bf16[32,16,384]{2,1,0:T(8,128)(2,1)S(1)}, u32[]{:S(2)}, u32[]{:S(2)}) async-start(bf16[32,16,384]{2,1,0:T(8,128)(2,1)} %bitcast.15), calls=%async_computation | async-start | bytes 786432 | tf_op jit(solution)/shard_map/all_to_all | solution.py:217
  133.9 1.4 fusion.4
  135.3 1.4 fusion.6
  136.7 1.4 fusion.8
  138.0 1.4 fusion.10
  139.4 1.4 fusion.14
  140.8 1.4 fusion.16
  142.2 1.4 fusion.2
  143.5 6.3 %all-to-all-done.got_ref = bf16[32,16,384]{2,1,0:T(8,128)(2,1)S(1)} async-done(((bf16[32,16,384]{2,1,0:T(8,128)(2,1)}), bf16[32,16,384]{2,1,0:T(8,128)(2,1)S(1)}, u32[]{:S(2)}, u32[]{:S(2)}) %all-to-all-start) | async-done | bytes 393248 | tf_op jit(solution)/shard_map/all_to_all | solution.py:217
  149.9 0.8 copy-done.3
  150.6 2.0 %merge.1 = bf16[32,16,128]{2,1,0:T(8,128)(2,1)} custom-call(bf16[32,16,384]{2,1,0:T(8,128)(2,1)} %copy-done.3), custom_call_target="tpu_custom_call" | custom-call | tf_op jit(solution)/shard_map/merge/pallas_call | solution.py:218
  152.7 4.3 %all-to-all-start.1 = ((bf16[32,16,128]{2,1,0:T(8,128)(2,1)}), bf16[32,16,128]{2,1,0:T(8,128)(2,1)S(1)}, u32[]{:S(2)}, u32[]{:S(2)}) async-start(bf16[32,16,128]{2,1,0:T(8,128)(2,1)} %merge.1), calls=%async_computation.1 | async-start | bytes 262144 | tf_op jit(solution)/shard_map/all_to_all | solution.py:223
  157.0 1.4 fusion.12
  158.4 9.1 %all-to-all-done.1 = bf16[32,16,128]{2,1,0:T(8,128)(2,1)S(1)} async-done(((bf16[32,16,128]{2,1,0:T(8,128)(2,1)}), bf16[32,16,128]{2,1,0:T(8,128)(2,1)S(1)}, u32[]{:S(2)}, u32[]{:S(2)}) %all-to-all-start.1) | async-done | bytes 131104 | tf_op jit(solution)/shard_map/all_to_all | solution.py:223
  (50 shorter events, 3.3 us)
Async XLA Ops:
  6.5 91.0 %all-gather.5.cloned.1.call-start = ((), (), s32[]{:S(2)}) async-start(), calls=%async_computation.2 | async-start | bytes 4718592 | tf_op jit(solution)/shard_map/all_gather | solution.py:157
  6.5 58.9 %collective-permute-start.5 = (bf16[512,2048]{1,0:T(8,128)(2,1)}, bf16[512,2048]{1,0:T(8,128)(2,1)}, u32[]{:S(2)}, u32[]{:S(2)}) collective-permute-start(bf16[512,2048]{1,0:T(8,128)(2,1)} %refs_0_.1), channel_id=1, source_target_pairs={{0,2},{2,4},{4,6},{6,0},{1,3},{3,5},{5,7},{7,1},{8,10},{10,12},{12... | collective-permute-start | bytes 6291464 | tf_op jit(solution)/shard_map/ppermute | solution.py:20
  8.1 57.4 %collective-permute-start.6 = (bf16[512,2048]{1,0:T(8,128)(2,1)}, bf16[512,2048]{1,0:T(8,128)(2,1)}, u32[]{:S(2)}, u32[]{:S(2)}) collective-permute-start(bf16[512,2048]{1,0:T(8,128)(2,1)} %refs_0_.1), channel_id=1, source_target_pairs={{0,6},{2,0},{4,2},{6,4},{1,7},{3,1},{5,3},{7,5},{8,14},{10,8},{12,... | collective-permute-start | bytes 6291464 | tf_op jit(solution)/shard_map/ppermute | solution.py:20
  8.7 15.7 %collective-permute-start = (bf16[128,512]{1,0:T(8,128)(2,1)}, bf16[128,512]{1,0:T(8,128)(2,1)S(1)}, u32[]{:S(2)}, u32[]{:S(2)}) collective-permute-start(bf16[128,512]{1,0:T(8,128)(2,1)} %param.6), channel_id=1, source_target_pairs={{0,0},{1,32},{2,64},{3,96},{4,128},{5,160},{6,192},{7,224},{8,8},{... | collective-permute-start | bytes 393224 | tf_op jit(solution)/shard_map/ppermute | solution.py:35
  24.4 7.2 %collective-permute-start.1 = (bf16[128,512]{1,0:T(8,128)(2,1)S(1)}, bf16[128,512]{1,0:T(8,128)(2,1)S(1)}, u32[]{:S(2)}, u32[]{:S(2)}) collective-permute-start(bf16[128,512]{1,0:T(8,128)(2,1)S(1)} %collective-permute-done), channel_id=1, source_target_pairs={{0,8},{8,16},{16,24},{24,0},{1,9},{9,17},{17,25},{25,1},{2,10},{10... | collective-permute-start | bytes 393224 | tf_op jit(solution)/shard_map/ppermute | solution.py:20
  25.9 5.7 %collective-permute-start.2 = (bf16[128,512]{1,0:T(8,128)(2,1)S(1)}, bf16[128,512]{1,0:T(8,128)(2,1)S(1)}, u32[]{:S(2)}, u32[]{:S(2)}) collective-permute-start(bf16[128,512]{1,0:T(8,128)(2,1)S(1)} %collective-permute-done), channel_id=1, source_target_pairs={{0,24},{8,0},{16,8},{24,16},{1,25},{9,1},{17,9},{25,17},{2,26},{10... | collective-permute-start | bytes 393224 | tf_op jit(solution)/shard_map/ppermute | solution.py:20
  27.6 6.5 %collective-permute-start.3 = (bf16[128,512]{1,0:T(8,128)(2,1)S(1)}, bf16[128,512]{1,0:T(8,128)(2,1)S(1)}, u32[]{:S(2)}, u32[]{:S(2)}) collective-permute-start(bf16[128,512]{1,0:T(8,128)(2,1)S(1)} %collective-permute-done), channel_id=1, source_target_pairs={{0,16},{8,24},{16,0},{24,8},{1,17},{9,25},{17,1},{25,9},{2,18},{10... | collective-permute-start | bytes 393224 | tf_op jit(solution)/shard_map/ppermute | solution.py:20
  34.1 0.8 copy-start.2
  35.0 59.4 %copy-start.6 = (s32[512]{0:T(512)S(1)}, s32[512]{0:T(512)}, u32[]{:S(2)}) copy-start(s32[512]{0:T(512)} %param.10) | copy-start | bytes 6148
  35.0 59.6 %copy-start.7 = (s32[1,8]{1,0:T(1,128)S(1)}, s32[1,8]{1,0:T(1,128)}, u32[]{:S(2)}) copy-start(s32[1,8]{1,0:T(1,128)} %param.11) | copy-start | bytes 100
  35.0 98.9 %all-gather.7.cloned.1.call-start = ((), (), s32[]{:S(2)}) async-start(), calls=%async_computation.3 | async-start | bytes 1179648 | tf_op jit(solution)/shard_map/all_gather | solution.py:155
  35.0 62.4 %collective-permute-start.7 = (bf16[512,2048]{1,0:T(8,128)(2,1)}, bf16[512,2048]{1,0:T(8,128)(2,1)}, u32[]{:S(2)}, u32[]{:S(2)}) collective-permute-start(bf16[512,2048]{1,0:T(8,128)(2,1)} %refs_0_.1), channel_id=1, source_target_pairs={{0,1},{1,0},{2,3},{3,2},{4,5},{5,4},{6,7},{7,6},{8,9},{9,8},{10,11... | collective-permute-start | bytes 6291464 | tf_op jit(solution)/shard_map/ppermute | solution.py:20
  35.1 33.4 %collective-permute-start.4 = (bf16[512,128]{1,0:T(8,128)(2,1)}, bf16[512,128]{1,0:T(8,128)(2,1)S(1)}, u32[]{:S(2)}, u32[]{:S(2)}) collective-permute-start(bf16[512,128]{1,0:T(8,128)(2,1)} %param.8), channel_id=1, source_target_pairs={{0,0},{1,32},{2,64},{3,96},{4,128},{5,160},{6,192},{7,224},{8,8},{... | collective-permute-start | bytes 393224 | tf_op jit(solution)/shard_map/ppermute | solution.py:35
  65.5 32.0 %collective-permute-start.8 = (bf16[512,2048]{1,0:T(8,128)(2,1)}, bf16[512,2048]{1,0:T(8,128)(2,1)}, u32[]{:S(2)}, u32[]{:S(2)}) collective-permute-start(bf16[512,2048]{1,0:T(8,128)(2,1)} %collective-permute-done.5.refs_1_.up_ref), channel_id=1, source_target_pairs={{0,1},{1,0},{2,3},{3,2},{4,5},{5,4},{6,7},{7,6},{8,9},{9,8},{10,11... | collective-permute-start | bytes 6291464 | tf_op jit(solution)/shard_map/ppermute | solution.py:20
  65.5 32.0 %collective-permute-start.9 = (bf16[512,2048]{1,0:T(8,128)(2,1)}, bf16[512,2048]{1,0:T(8,128)(2,1)}, u32[]{:S(2)}, u32[]{:S(2)}) collective-permute-start(bf16[512,2048]{1,0:T(8,128)(2,1)} %collective-permute-done.6.refs_2_.down_ref), channel_id=1, source_target_pairs={{0,1},{1,0},{2,3},{3,2},{4,5},{5,4},{6,7},{7,6},{8,9},{9,8},{10,11... | collective-permute-start | bytes 6291464 | tf_op jit(solution)/shard_map/ppermute | solution.py:20
  68.6 29.0 %copy-start = (bf16[512,2048]{1,0:T(8,128)(2,1)S(1)}, bf16[512,2048]{1,0:T(8,128)(2,1)}, u32[]{:S(2)}) copy-start(bf16[512,2048]{1,0:T(8,128)(2,1)} %refs_0_.1) | copy-start | bytes 6291460
  68.6 25.3 %collective-permute-start.10 = (bf16[256,2048]{1,0:T(8,128)(2,1)}, bf16[256,2048]{1,0:T(8,128)(2,1)S(1)}, u32[]{:S(2)}, u32[]{:S(2)}) collective-permute-start(bf16[256,2048]{1,0:T(8,128)(2,1)} %get-tuple-element.7), channel_id=1, source_target_pairs={{0,2},{2,4},{4,6},{6,0},{1,3},{3,5},{5,7},{7,1},{8,10},{10,12},{12... | collective-permute-start | bytes 3145736 | tf_op jit(solution)/shard_map/ppermute | solution.py:20
  68.6 2.0 %copy-start.4 = (bf16[512,128]{1,0:T(8,128)(2,1)}, bf16[512,128]{1,0:T(8,128)(2,1)S(1)}, u32[]{:S(2)}) copy-start(bf16[512,128]{1,0:T(8,128)(2,1)S(1)} %collective-permute-done.4) | copy-start | bytes 393220
  68.6 25.5 %collective-permute-start.11 = (bf16[256,2048]{1,0:T(8,128)(2,1)}, bf16[256,2048]{1,0:T(8,128)(2,1)}, u32[]{:S(2)}, u32[]{:S(2)}) collective-permute-start(bf16[256,2048]{1,0:T(8,128)(2,1)} %get-tuple-element.8), channel_id=1, source_target_pairs={{0,6},{2,0},{4,2},{6,4},{1,7},{3,1},{5,3},{7,5},{8,14},{10,8},{12,... | collective-permute-start | bytes 3145736 | tf_op jit(solution)/shard_map/ppermute | solution.py:20
  93.9 16.0 %collective-permute-start.12 = (bf16[256,2048]{1,0:T(8,128)(2,1)S(1)}, bf16[256,2048]{1,0:T(8,128)(2,1)}, u32[]{:S(2)}, u32[]{:S(2)}) collective-permute-start(bf16[256,2048]{1,0:T(8,128)(2,1)S(1)} %collective-permute-done.10.refs_0_), channel_id=1, source_target_pairs={{0,1},{1,0},{2,3},{3,2},{4,5},{5,4},{6,7},{7,6},{8,9},{9,8},{10,11... | collective-permute-start | bytes 3145736 | tf_op jit(solution)/shard_map/ppermute | solution.py:20
  94.1 15.8 %collective-permute-start.13 = (bf16[256,2048]{1,0:T(8,128)(2,1)}, bf16[256,2048]{1,0:T(8,128)(2,1)}, u32[]{:S(2)}, u32[]{:S(2)}) collective-permute-start(bf16[256,2048]{1,0:T(8,128)(2,1)} %collective-permute-done.11.refs_1_), channel_id=1, source_target_pairs={{0,1},{1,0},{2,3},{3,2},{4,5},{5,4},{6,7},{7,6},{8,9},{9,8},{10,11... | collective-permute-start | bytes 3145736 | tf_op jit(solution)/shard_map/ppermute | solution.py:20
  97.5 12.3 %copy-start.1 = (bf16[2048,128]{1,0:T(8,128)(2,1)S(1)}, bf16[2048,128]{1,0:T(8,128)(2,1)}, u32[]{:S(2)}) copy-start(bf16[2048,128]{1,0:T(8,128)(2,1)} %proj_ref.1) | copy-start | bytes 1572868
  121.5 28.4 %all-to-all-start = ((bf16[32,16,384]{2,1,0:T(8,128)(2,1)}), bf16[32,16,384]{2,1,0:T(8,128)(2,1)S(1)}, u32[]{:S(2)}, u32[]{:S(2)}) async-start(bf16[32,16,384]{2,1,0:T(8,128)(2,1)} %bitcast.15), calls=%async_computation | async-start | bytes 786432 | tf_op jit(solution)/shard_map/all_to_all | solution.py:217
  133.9 33.7 %copy-start.5 = (f32[512,8]{0,1:T(8,128)S(1)}, f32[512,8]{0,1:T(8,128)}, u32[]{:S(2)}) copy-start(f32[512,8]{0,1:T(8,128)} %convert_divide_fusion) | copy-start | bytes 49156
  149.9 0.8 copy-start.3
  152.7 14.8 %all-to-all-start.1 = ((bf16[32,16,128]{2,1,0:T(8,128)(2,1)}), bf16[32,16,128]{2,1,0:T(8,128)(2,1)S(1)}, u32[]{:S(2)}, u32[]{:S(2)}) async-start(bf16[32,16,128]{2,1,0:T(8,128)(2,1)} %merge.1), calls=%async_computation.1 | async-start | bytes 262144 | tf_op jit(solution)/shard_map/all_to_all | solution.py:223
Sparse Core Ops, SparseCore 0:
  35.1 55.4 all-gather.4
  92.4 40.0 all-gather.6

commit v3 on v2

--- a/solution.py
+++ b/solution.py
@@ -9,8 +9,8 @@
 
 TILE = 512
 FA = 1 << 20
-FB = 1 << 20
 SLICE = 1 << 36
+BLOCK = 1 << 20
 F32 = jnp.float32
 BF16 = jnp.bfloat16
 
@@ -37,11 +37,32 @@
 
 def along_x(block):
     x = lax.axis_index("x")
-    out = jnp.zeros((512, 512), BF16)
+    out = jnp.zeros((544, 512), BF16)
     for by in (0, 1, 3, 2):
         got = block if by == 0 else shift(block, "x", by)
         out = lax.dynamic_update_slice(out, got, (((x - by) % 4) * 128, 0))
     return out
+
+
+def block_kernel(x_ref, hidden_ref, proj_in_ref, out_ref):
+    row = lax.broadcasted_iota(jnp.int32, (32, 128), 0)
+    column = lax.broadcasted_iota(jnp.int32, (32, 128), 1)
+    chosen = (column == (row // 4) * 16 + row % 4 + 4 * x_ref[0]).astype(BF16)
+    out_ref[:128] = hidden_ref[...]
+    out_ref[128:] = lax.dot_general(
+        chosen, proj_in_ref[...], (((1,), (1,)), ((), ())), preferred_element_type=F32
+    ).astype(BF16)
+
+
+def with_columns(hidden, proj_in, x):
+    return pl.pallas_call(
+        block_kernel,
+        out_shape=jax.ShapeDtypeStruct((160, 512), BF16),
+        in_specs=[pl.BlockSpec(memory_space=pltpu.SMEM)] + [pl.BlockSpec(memory_space=pltpu.VMEM)] * 2,
+        out_specs=pl.BlockSpec(memory_space=pltpu.VMEM),
+        cost_estimate=pl.CostEstimate(flops=BLOCK, bytes_accessed=1 << 20, transcendentals=0),
+        name="block",
+    )(x.astype(jnp.int32).reshape(1), hidden, proj_in)
 
 
 def halves_kernel(up_ref, down_ref, early_ref, a_ref, b_ref):
@@ -67,21 +88,17 @@
     )(up, down, early)
 
 
-def dots(hid_ref, slot_ref, pieces, refs, acc):
+def dots(hid_ref, slot_ref, pieces, refs):
+    acc = None
     for ref, (place, low, rows) in zip(refs, pieces):
         part = jnp.dot(
-            hid_ref[slot_ref[place], :, low : low + rows], ref[...], preferred_element_type=F32
+            hid_ref[slot_ref[place], :512, low : low + rows], ref[...], preferred_element_type=F32
         )
         acc = part if acc is None else acc + part
     return acc
 
 
-def first_kernel(pieces, slot_ref, hid_ref, *refs):
-    heads, part_ref = refs[: len(pieces)], refs[len(pieces)]
-    part_ref[...] = dots(hid_ref, slot_ref, pieces, heads, None)
-
-
-def last_kernel(pieces, slot_ref, hid_ref, part_ref, proj_ref, tgt_ref, rows_ref, *refs):
+def head_kernel(pieces, slot_ref, hid_ref, proj_ref, tgt_ref, rows_ref, *refs):
     heads, (out_ref, max_ref, rest_ref, hit_ref, sum_ref) = refs[: len(pieces)], refs[len(pieces) :]
     step = pl.program_id(0)
 
@@ -92,7 +109,7 @@
         hit_ref[...] = jnp.zeros_like(hit_ref)
         sum_ref[...] = jnp.zeros_like(sum_ref)
 
-    logits = dots(hid_ref, slot_ref, pieces, heads, part_ref[...])
+    logits = dots(hid_ref, slot_ref, pieces, heads)
     old = max_ref[...]
     new = jnp.maximum(old, jnp.max(logits, axis=1, keepdims=True))
     scale = jnp.exp(old - new)
@@ -121,6 +138,17 @@
         out_ref[:, 128:256] = jnp.where(term == 0, high, jnp.where(term == 1, middle, low)).astype(BF16)
 
 
+def project_kernel(hid_ref, out_ref, sum_ref):
+    @pl.when(pl.program_id(0) == 0)
+    def _():
+        sum_ref[...] = jnp.zeros_like(sum_ref)
+
+    sum_ref[...] += lax.dot_general(
+        hid_ref[0, 512:], hid_ref[0, :512], (((1,), (1,)), ((), ())), preferred_element_type=F32
+    )
+    out_ref[...] = sum_ref[...].astype(BF16)
+
+
 def merge_kernel(got_ref, out_ref):
     terms = got_ref[:, :, 128:256].astype(F32)
     top, rest, hit = (
@@ -136,6 +164,22 @@
     out_ref[...] = jnp.broadcast_to(merged[None], out_ref.shape)
 
 
+def final_kernel(lengths_ref, in_ref, rows_ref, out_ref):
+    position = lax.broadcasted_iota(jnp.int32, (16, 512), 1)
+    columns = in_ref[...]
+    start = 0
+    masked = []
+    for e in range(8):
+        end = start + lengths_ref[0, e]
+        inside = jnp.logical_and(position >= start, position < end)
+        masked.append(jnp.where(inside, columns, jnp.zeros_like(columns)))
+        start = end
+    summed = jnp.dot(jnp.concatenate(masked, axis=0), rows_ref[...], preferred_element_type=F32)
+    for e in range(8):
+        length = jnp.full((4, 128), lengths_ref[0, e], jnp.int32).astype(F32)
+        out_ref[e] = summed[16 * e : 16 * e + 4] / length
+
+
 PARAMS = dict(dimension_semantics=("arbitrary",), vmem_limit_bytes=48 << 20)
 
 
@@ -152,10 +196,10 @@
     me = z * 4 + x
 
     up, down = shift(head, "y", 1), shift(head, "y", -1)
-    pin = lax.all_gather(exchange_corners(proj_in), "z", axis=0, tiled=False)
-    mine = along_x(exchange_corners(hidden_states))
+    block = exchange_corners(with_columns(hidden_states, proj_in, x))
+    mine = lax.dynamic_update_slice(along_x(block[:128]), block[128:], (512, 0))
     hid = lax.all_gather(mine, "z", axis=0, tiled=False)
-    far_a, far_b = halves(up, down, mine)
+    far_a, far_b = halves(up, down, block)
     far_a, far_b = shift(far_a, "y", 1), shift(far_b, "y", -1)
 
     local_target = targets[:, None] - me * 2048
@@ -165,75 +209,64 @@
     def slot(dy, dc):
         return ((y + dy) % 4) * 2 + (c + dc) % 2
 
-    near = [(head, 0, 0, 512), (up, 1, 0, 512), (down, 2, 0, 512)]
-    far = [(far_a, 0, 0, 256), (far_b, 0, 256, 256)]
-
-    def both(items, count):
-        refs = [i[0] for i in items] + [swap(i[0]) for i in items]
-        pieces = [i[1:] for i in items] + [(i[1] + count, i[2], i[3]) for i in items]
-        return refs, pieces
-
-    near_refs, near_pieces = both(near, 3)
-    far_refs, far_pieces = both(far, 1)
-    near_slots = jnp.stack([slot(dy, dc) for dc in (0, 1) for dy in (0, -1, 1)]).astype(jnp.int32)
-    far_slots = jnp.stack([slot(2, dc) for dc in (0, 1)]).astype(jnp.int32)
-
-    part = pl.pallas_call(
-        functools.partial(first_kernel, near_pieces),
-        out_shape=jax.ShapeDtypeStruct((512, 2048), F32),
-        grid_spec=pltpu.PrefetchScalarGridSpec(
-            num_scalar_prefetch=1,
-            grid=(2048 // TILE,),
-            in_specs=[whole((8, 512, 512))] + [head_spec(r) for r in near_refs],
-            out_specs=pl.BlockSpec((512, TILE), lambda i, s: (0, i)),
-        ),
-        compiler_params=pltpu.CompilerParams(**PARAMS),
-        cost_estimate=pl.CostEstimate(flops=FA, bytes_accessed=1 << 20, transcendentals=0),
-        name="first_slices",
-    )(near_slots, hid, *near_refs)
+    items = [(head, 0, 0, 512), (up, 1, 0, 512), (down, 2, 0, 512)]
+    items += [(far_a, 3, 0, 256), (far_b, 3, 256, 256)]
+    refs = [i[0] for i in items] + [swap(i[0]) for i in items]
+    pieces = [i[1:] for i in items] + [(i[1] + 4, i[2], i[3]) for i in items]
+    slots = jnp.stack([slot(dy, dc) for dc in (0, 1) for dy in (0, -1, 1, 2)]).astype(jnp.int32)
 
     out = pl.pallas_call(
-        functools.partial(last_kernel, far_pieces),
+        functools.partial(head_kernel, pieces),
         out_shape=jax.ShapeDtypeStruct((512, 384), BF16),
         grid_spec=pltpu.PrefetchScalarGridSpec(
             num_scalar_prefetch=1,
             grid=(2048 // TILE,),
             in_specs=[
-                whole((8, 512, 512)),
-                pl.BlockSpec((512, TILE), lambda i, s: (0, i)),
+                whole((8, 544, 512)),
                 pl.BlockSpec((TILE, 128), lambda i, s: (i, 0)),
                 whole((512, 1)),
                 whole((512, 128)),
             ]
-            + [head_spec(r) for r in far_refs],
+            + [head_spec(r) for r in refs],
             out_specs=whole((512, 384)),
             scratch_shapes=[pltpu.VMEM((512, 1), F32)] * 3 + [pltpu.VMEM((512, 128), F32)],
         ),
         compiler_params=pltpu.CompilerParams(**PARAMS),
-        cost_estimate=pl.CostEstimate(flops=FB, bytes_accessed=1 << 20, transcendentals=0),
-        name="last_slices",
-    )(far_slots, hid, part, proj_out, local_target, rows, *far_refs)
+        cost_estimate=pl.CostEstimate(flops=FA, bytes_accessed=1 << 20, transcendentals=0),
+        name="head",
+    )(slots, hid, proj_out, local_target, rows, *refs)
 
     got = lax.all_to_all(out, ("z", "x"), 0, 0, tiled=True).reshape(32, 16, 384)
+    in_proj = pl.pallas_call(
+        project_kernel,
+        out_shape=jax.ShapeDtypeStruct((32, 512), BF16),
+        grid=(8,),
+        in_specs=[
+            pl.BlockSpec((1, 544, 512), lambda i: (i, 0, 0)),
+        ],
+        out_specs=pl.BlockSpec((32, 512), lambda i: (0, 0)),
+        scratch_shapes=[pltpu.VMEM((32, 512), F32)],
+        cost_estimate=pl.CostEstimate(flops=1 << 30, bytes_accessed=4 << 20, transcendentals=0),
+        name="project",
+    )(hid)
+    in_proj = lax.dynamic_slice_in_dim(in_proj, 4 * z, 4, 0)
+    in_proj = jnp.concatenate([in_proj, jnp.zeros((12, 512), BF16)], axis=0)
+    in_vmem = pl.BlockSpec(memory_space=pltpu.VMEM)
     merged = pl.pallas_call(
         merge_kernel,
         out_shape=jax.ShapeDtypeStruct((32, 16, 128), BF16),
+        in_specs=[in_vmem],
+        out_specs=in_vmem,
         name="merge",
     )(got)
-    out_proj = lax.all_to_all(merged, ("z", "x"), 0, 0, tiled=True).reshape(512, 128).astype(F32)
-
-    seq_lengths = lengths[0]
-    ends = jnp.cumsum(seq_lengths)
-    starts = ends - seq_lengths
-    positions = jnp.arange(512, dtype=jnp.int32)
-    member = (
-        (positions[:, None] >= starts[None, :]) & (positions[:, None] < ends[None, :])
-    ).astype(F32)
-    membership = member / seq_lengths.astype(F32)[None, :]
-    in_proj = sum(jnp.dot(hid[d], pin[d], preferred_element_type=F32) for d in range(8)).astype(BF16)
-    in_slice = lax.dynamic_slice_in_dim(in_proj, me * 4, 4, 1)
-    expanded = membership[:, :, None] * in_slice.astype(F32)[:, None, :]
-    return jnp.einsum("ter,tc->erc", expanded, out_proj, precision=lax.Precision.HIGHEST)
+    out_proj = lax.all_to_all(merged, ("z", "x"), 0, 0, tiled=True).reshape(512, 128)
+    return pl.pallas_call(
+        final_kernel,
+        out_shape=jax.ShapeDtypeStruct((8, 4, 128), F32),
+        in_specs=[pl.BlockSpec(memory_space=pltpu.SMEM), in_vmem, in_vmem],
+        out_specs=in_vmem,
+        name="final",
+    )(lengths, in_proj, out_proj)
 
 
 def solution(mesh):

time: 176 us -> 169 us (0.960)
  blocking collectives: 0 us -> 22.4 us
  starting transfers between devices: 34.9 us -> 22 us
  matrix products: 13 us -> 1.89 us
  waiting for transfers between devices: 81.5 us -> 70.6 us
  Pallas kernels: 28.6 us -> 32.4 us
  local copies, waits for them, and re-layouts: 2.55 us -> 5.51 us
    all_to_all x0 -> x1, blocking collectives: none -> 22.4 us  [local(): got = lax.all_to_all(out, ('z', 'x'), 0, 0, tiled=True).reshape(32, 16, 384)]
    all_to_all x1 -> x0, starting transfers between devices: 12.4 us -> none  [local(): got = lax.all_to_all(out, ('z', 'x'), 0, 0, tiled=True).reshape(32, 16, 384)]
    dot_general x9 -> x0, matrix products: 11.1 us -> none  [the longest x8 11 us: local(): jnp.dot(hid[d], pin[d], preferred_element_type=F32)]
    all_gather x1, waiting for transfers between devices: 0.02 us -> 7.37 us  [local(): hid = lax.all_gather(mine, 'z', axis=0, tiled=False)]
    all_to_all x1 -> x0, waiting for transfers between devices: 6.32 us -> none  [local(): got = lax.all_to_all(out, ('z', 'x'), 0, 0, tiled=True).reshape(32, 16, 384)]
    ppermute x12, waiting for transfers between devices: 56.4 us -> 50.1 us  [shift(): return lax.ppermute(x, axis, [(i, (i + by) % n) for i in range(n)])]
    all_to_all x1, waiting for transfers between devices: 9.13 us -> 2.94 us  [local(): lax.all_to_all(merged, ('z', 'x'), 0, 0, tiled=True).reshape(512, 128)]
    pallas_call x2 -> x4, Pallas kernels: 23.9 us -> 27.7 us  [the longest x1 18 us: local(): pl.pallas_call(functools.partial(head_kernel, pieces), out_shape=jax.Shap...]
  transfers between devices with their start and end apart: 18 -> 15, of which waited for: 8 -> 9; matrix products, arithmetic and copies ran while one was open for 8% -> 2% of each run, Pallas kernels for 15% -> 6%
where the time goes in v3:
time: 169 us; the launch traced here: 168 us
  waiting for transfers between devices  70.6 us (42%)
  Pallas kernels  32.4 us (19%)
  blocking collectives  22.4 us (13%)
  starting transfers between devices  22 us (13%)
  between operations  13.5 us (8%)
  local copies, waits for them, and re-layouts  5.51 us (3%)
  matrix products  1.89 us (1%)
    ppermute x12, waiting for transfers between devices, shift(): return lax.ppermute(x, axis, [(i, (i + by) % n) for i in range(n)])  50.1 us
    all_to_all x1, blocking collectives, local(): got = lax.all_to_all(out, ('z', 'x'), 0, 0, tiled=True).reshape(32, 16, 384)  22.4 us
    pallas_call x1, Pallas kernels, local(): pl.pallas_call(functools.partial(head_kernel, pieces), out_shape=jax.Shap...  18 us
    ppermute x12, starting transfers between devices, shift(): return lax.ppermute(x, axis, [(i, (i + by) % n) for i in range(n)])  11.7 us
    ppermute x1, waiting for transfers between devices, exchange_corners(): return lax.ppermute(x, ('z', 'x', 'y', 'c'), pairs)  10.2 us
    all_gather x1, waiting for transfers between devices, local(): hid = lax.all_gather(mine, 'z', axis=0, tiled=False)  7.37 us
    pallas_call x1, Pallas kernels, local(): pl.pallas_call(project_kernel, out_shape=jax.ShapeDtypeStruct((32, 512),...  6.29 us
    ppermute x1, starting transfers between devices, exchange_corners(): return lax.ppermute(x, ('z', 'x', 'y', 'c'), pairs)  6.1 us
  transfers between devices with their start and end apart: 15, of which 9 were waited for; matrix products, arithmetic and copies ran while one was open for 2% of the time, Pallas kernels for 6%

profile of v3, /device:TPU:8, one launch (start us, length us, event | category | flops | bytes accessed | tf_op | source)
XLA Modules:
  0.0 168.4 jit_solution(12954657398106547931)
XLA Ops:
  6.5 1.6 collective-permute-start.4
  8.1 0.6 collective-permute-start.5
  8.7 1.8 %block.1 = bf16[160,512]{1,0:T(8,128)(2,1)} custom-call(s32[1]{0:T(128)} %bitcast.x_ref, bf16[128,512]{1,0:T(8,128)(2,1)} %hidden_ref.1, bf16[512,128]{1,0:T(8,128)(2,1)} %proj_in_ref.1), custom_call_target="tpu_custom_call" | custom-call | flops 1048576 | bytes 1048576 | tf_op jit(solution)/shard_map/block/pallas_call | solution.py:58
  10.5 6.1 %collective-permute-start = (bf16[160,512]{1,0:T(8,128)(2,1)}, bf16[160,512]{1,0:T(8,128)(2,1)S(1)}, u32[]{:S(2)}, u32[]{:S(2)}) collective-permute-start(bf16[160,512]{1,0:T(8,128)(2,1)} %block.1), channel_id=1, source_target_pairs={{0,0},{1,32},{2,64},{3,96},{4,128},{5,160},{6,192},{7,224},{8,8},{... | collective-permute-start | bytes 491528 | tf_op jit(solution)/shard_map/ppermute | solution.py:35
  16.6 1.6 collective-permute-start.8
  18.2 10.2 %collective-permute-done.early_ref = bf16[160,512]{1,0:T(8,128)(2,1)S(1)} collective-permute-done((bf16[160,512]{1,0:T(8,128)(2,1)}, bf16[160,512]{1,0:T(8,128)(2,1)S(1)}, u32[]{:S(2)}, u32[]{:S(2)}) %collective-permute-start) | collective-permute-done | bytes 163872 | tf_op jit(solution)/shard_map/ppermute | solution.py:35
  28.4 1.6 collective-permute-start.1
  29.9 1.7 %collective-permute-start.2 = (bf16[128,512]{1,0:T(8,128)(2,1)S(1)}, bf16[128,512]{1,0:T(8,128)(2,1)S(1)}, u32[]{:S(2)}, u32[]{:S(2)}) collective-permute-start(bf16[128,512]{1,0:T(8,128)(2,1)S(1)} %slice.8), channel_id=1, source_target_pairs={{0,24},{8,0},{16,8},{24,16},{1,25},{9,1},{17,9},{25,17},{2,26},{10... | collective-permute-start | bytes 393224 | tf_op jit(solution)/shard_map/ppermute | solution.py:20
  31.8 3.1 %collective-permute-done.1 = bf16[128,512]{1,0:T(8,128)(2,1)S(1)} collective-permute-done((bf16[128,512]{1,0:T(8,128)(2,1)S(1)}, bf16[128,512]{1,0:T(8,128)(2,1)S(1)}, u32[]{:S(2)}, u32[]{:S(2)}) %collective-permute-start.1) | collective-permute-done | bytes 131104 | tf_op jit(solution)/shard_map/ppermute | solution.py:20
  34.9 1.6 collective-permute-start.3
  36.5 4.8 %collective-permute-done.3 = bf16[128,512]{1,0:T(8,128)(2,1)S(1)} collective-permute-done((bf16[128,512]{1,0:T(8,128)(2,1)S(1)}, bf16[128,512]{1,0:T(8,128)(2,1)S(1)}, u32[]{:S(2)}, u32[]{:S(2)}) %collective-permute-start.3) | collective-permute-done | bytes 131104 | tf_op jit(solution)/shard_map/ppermute | solution.py:20
  41.4 0.8 copy-done.1
  42.2 18.9 %collective-permute-done.4.up_ref.refs_1_ = bf16[512,2048]{1,0:T(8,128)(2,1)S(1)} collective-permute-done((bf16[512,2048]{1,0:T(8,128)(2,1)}, bf16[512,2048]{1,0:T(8,128)(2,1)S(1)}, u32[]{:S(2)}, u32[]{:S(2)}) %collective-permute-start.4) | collective-permute-done | bytes 2097184 | tf_op jit(solution)/shard_map/ppermute | solution.py:20
  61.2 1.4 copy-done.2
  62.5 2.6 %halves.1 = (bf16[256,2048]{1,0:T(8,128)(2,1)}, bf16[256,2048]{1,0:T(8,128)(2,1)}) custom-call(bf16[512,2048]{1,0:T(8,128)(2,1)} %copy-done.2, bf16[512,2048]{1,0:T(8,128)(2,1)} %collective-permute-done.5.down_ref.refs_2_, bf16[160,512]{1,0:T(8,128)(2,1)} %copy-done.3), custom_call_target="tpu_custom_call" | custom-call | flops 68719476736 | bytes 4194304 | tf_op jit(solution)/shard_map/halves/pallas_call | solution.py:76
  65.1 2.0 %collective-permute-start.7 = (bf16[256,2048]{1,0:T(8,128)(2,1)}, bf16[256,2048]{1,0:T(8,128)(2,1)S(1)}, u32[]{:S(2)}, u32[]{:S(2)}) collective-permute-start(bf16[256,2048]{1,0:T(8,128)(2,1)} %get-tuple-element.8), channel_id=1, source_target_pairs={{0,6},{2,0},{4,2},{6,4},{1,7},{3,1},{5,3},{7,5},{8,14},{10,8},{12,... | collective-permute-start | bytes 3145736 | tf_op jit(solution)/shard_map/ppermute | solution.py:20
  67.2 0.5 collective-permute-start.9
  67.7 21.6 %collective-permute-done.6.refs_3_ = bf16[256,2048]{1,0:T(8,128)(2,1)S(1)} collective-permute-done((bf16[256,2048]{1,0:T(8,128)(2,1)}, bf16[256,2048]{1,0:T(8,128)(2,1)S(1)}, u32[]{:S(2)}, u32[]{:S(2)}) %collective-permute-start.6) | collective-permute-done | bytes 1048608 | tf_op jit(solution)/shard_map/ppermute | solution.py:20
  90.0 1.9 %fusion.2.rows_ref = bf16[512,128]{1,0:T(8,128)(2,1)S(1)} fusion(bf16[2048,128]{1,0:T(8,128)(2,1)} %proj_ref.1, s32[512]{0:T(512)S(1)} %broadcast_subtract_fusion), kind=kOutput, calls=%fused_computation.3 | convolution fusion | flops 269549568 | bytes 657408 | tf_op jit(solution)/shard_map/dot_general | solution.py:207
  91.9 1.4 collective-permute-done.11.refs_8_
  93.6 7.4 %all-gather.2.cloned.1.call-done.hid_ref = bf16[8,544,512]{2,1,0:T(8,128)(2,1)} async-done(((bf16[1,544,512]{2,1,0:T(8,128)(2,1)}), bf16[8,544,512]{2,1,0:T(8,128)(2,1)}) %all-gather.2.cloned.1.call-update) | async-done | bytes 4456464 | tf_op jit(solution)/shard_map/all_gather | solution.py:201
  100.9 1.0 copy-done
  102.0 18.0 %head.1 = bf16[512,384]{1,0:T(8,128)(2,1)S(1)} custom-call(s32[8]{0:T(128)S(1)} %stack.35.slot_ref, bf16[8,544,512]{2,1,0:T(8,128)(2,1)} %all-gather.2.cloned.1.call-done.hid_ref, bf16[2048,128]{1,0:T(8,128)(2,1)S(1)} %copy-done, s32[512,1]{1,0:T(8,128)S(1)} %copy.8.tgt_ref, bf16[512,128]{1,0:T(8,128)(2,1)S(1)} %fusion.2.rows_ref, ...), custom_call_target="tpu_custom_call" | custom-call | flops 1048576 | bytes 1048576 | tf_op jit(solution)/shard_map/head/pallas_call | solution.py:218
  120.0 22.4 %all_to_all.14.got_ref = bf16[32,16,384]{2,1,0:T(8,128)(2,1)} all-to-all(bf16[32,16,384]{2,1,0:T(8,128)(2,1)S(1)} %bitcast.25), channel_id=1, replica_groups=mesh['z'=8,'x'=4,'y'=4,'c'=2] {'z','x'}, dimensions={0} | all-to-all | bytes 786432 | tf_op jit(solution)/shard_map/all_to_all | solution.py:239
  142.3 2.0 %merge.1 = bf16[32,16,128]{2,1,0:T(8,128)(2,1)} custom-call(bf16[32,16,384]{2,1,0:T(8,128)(2,1)} %all_to_all.14.got_ref), custom_call_target="tpu_custom_call" | custom-call | tf_op jit(solution)/shard_map/merge/pallas_call | solution.py:255
  144.4 4.2 %all-to-all-start.1 = ((bf16[32,16,128]{2,1,0:T(8,128)(2,1)}), bf16[32,16,128]{2,1,0:T(8,128)(2,1)S(1)}, u32[]{:S(2)}, u32[]{:S(2)}) async-start(bf16[32,16,128]{2,1,0:T(8,128)(2,1)} %merge.1), calls=%async_computation.1 | async-start | bytes 262144 | tf_op jit(solution)/shard_map/all_to_all | solution.py:262
  148.6 6.3 %project.1 = bf16[32,512]{1,0:T(8,128)(2,1)} custom-call(bf16[8,544,512]{2,1,0:T(8,128)(2,1)} %all-gather.2.cloned.1.call-done.hid_ref), custom_call_target="tpu_custom_call" | custom-call | flops 1073741824 | bytes 4194304 | tf_op jit(solution)/shard_map/project/pallas_call | solution.py:240
  154.9 0.7 constant_dynamic-slice_fusion
  155.6 0.6 concatenate.3.in_ref
  156.2 2.9 %all-to-all-done.1 = bf16[32,16,128]{2,1,0:T(8,128)(2,1)S(1)} async-done(((bf16[32,16,128]{2,1,0:T(8,128)(2,1)}), bf16[32,16,128]{2,1,0:T(8,128)(2,1)S(1)}, u32[]{:S(2)}, u32[]{:S(2)}) %all-to-all-start.1) | async-done | bytes 131104 | tf_op jit(solution)/shard_map/all_to_all | solution.py:262
  159.2 0.6 copy-done.4
  159.8 1.7 %final.1 = f32[8,4,128]{2,1,0:T(4,128)} custom-call(s32[1,8]{1,0:T(1,128)} %lengths_ref.1, bf16[16,512]{1,0:T(8,128)(2,1)} %concatenate.3.in_ref, bf16[512,128]{1,0:T(8,128)(2,1)} %bitcast.26), custom_call_target="tpu_custom_call" | custom-call | tf_op jit(solution)/shard_map/final/pallas_call | solution.py:263
  (31 shorter events, 1.1 us)
Async XLA Ops:
  6.5 94.4 %all-gather.2.cloned.1.call-start = ((), (), s32[]{:S(2)}) async-start(), calls=%async_computation.2 | async-start | bytes 5013504 | tf_op jit(solution)/shard_map/all_gather | solution.py:201
  6.5 54.6 %collective-permute-start.4 = (bf16[512,2048]{1,0:T(8,128)(2,1)}, bf16[512,2048]{1,0:T(8,128)(2,1)S(1)}, u32[]{:S(2)}, u32[]{:S(2)}) collective-permute-start(bf16[512,2048]{1,0:T(8,128)(2,1)} %refs_0_.1), channel_id=1, source_target_pairs={{0,2},{2,4},{4,6},{6,0},{1,3},{3,5},{5,7},{7,1},{8,10},{10,12},{12... | collective-permute-start | bytes 6291464 | tf_op jit(solution)/shard_map/ppermute | solution.py:20
  8.1 53.0 %collective-permute-start.5 = (bf16[512,2048]{1,0:T(8,128)(2,1)}, bf16[512,2048]{1,0:T(8,128)(2,1)}, u32[]{:S(2)}, u32[]{:S(2)}) collective-permute-start(bf16[512,2048]{1,0:T(8,128)(2,1)} %refs_0_.1), channel_id=1, source_target_pairs={{0,6},{2,0},{4,2},{6,4},{1,7},{3,1},{5,3},{7,5},{8,14},{10,8},{12,... | collective-permute-start | bytes 6291464 | tf_op jit(solution)/shard_map/ppermute | solution.py:20
  10.5 17.8 %collective-permute-start = (bf16[160,512]{1,0:T(8,128)(2,1)}, bf16[160,512]{1,0:T(8,128)(2,1)S(1)}, u32[]{:S(2)}, u32[]{:S(2)}) collective-permute-start(bf16[160,512]{1,0:T(8,128)(2,1)} %block.1), channel_id=1, source_target_pairs={{0,0},{1,32},{2,64},{3,96},{4,128},{5,160},{6,192},{7,224},{8,8},{... | collective-permute-start | bytes 491528 | tf_op jit(solution)/shard_map/ppermute | solution.py:35
  16.6 75.3 %collective-permute-start.8 = (bf16[512,2048]{1,0:T(8,128)(2,1)}, bf16[512,2048]{1,0:T(8,128)(2,1)}, u32[]{:S(2)}, u32[]{:S(2)}) collective-permute-start(bf16[512,2048]{1,0:T(8,128)(2,1)} %refs_0_.1), channel_id=1, source_target_pairs={{0,1},{1,0},{2,3},{3,2},{4,5},{5,4},{6,7},{7,6},{8,9},{9,8},{10,11... | collective-permute-start | bytes 6291464 | tf_op jit(solution)/shard_map/ppermute | solution.py:20
  28.4 32.8 %copy-start.3 = (bf16[160,512]{1,0:T(8,128)(2,1)}, bf16[160,512]{1,0:T(8,128)(2,1)S(1)}, u32[]{:S(2)}) copy-start(bf16[160,512]{1,0:T(8,128)(2,1)S(1)} %collective-permute-done.early_ref) | copy-start | bytes 491524
  28.4 6.5 %collective-permute-start.1 = (bf16[128,512]{1,0:T(8,128)(2,1)S(1)}, bf16[128,512]{1,0:T(8,128)(2,1)S(1)}, u32[]{:S(2)}, u32[]{:S(2)}) collective-permute-start(bf16[128,512]{1,0:T(8,128)(2,1)S(1)} %slice.8), channel_id=1, source_target_pairs={{0,8},{8,16},{16,24},{24,0},{1,9},{9,17},{17,25},{25,1},{2,10},{10... | collective-permute-start | bytes 393224 | tf_op jit(solution)/shard_map/ppermute | solution.py:20
  29.9 6.5 %collective-permute-start.2 = (bf16[128,512]{1,0:T(8,128)(2,1)S(1)}, bf16[128,512]{1,0:T(8,128)(2,1)S(1)}, u32[]{:S(2)}, u32[]{:S(2)}) collective-permute-start(bf16[128,512]{1,0:T(8,128)(2,1)S(1)} %slice.8), channel_id=1, source_target_pairs={{0,24},{8,0},{16,8},{24,16},{1,25},{9,1},{17,9},{25,17},{2,26},{10... | collective-permute-start | bytes 393224 | tf_op jit(solution)/shard_map/ppermute | solution.py:20
  34.9 6.5 %collective-permute-start.3 = (bf16[128,512]{1,0:T(8,128)(2,1)S(1)}, bf16[128,512]{1,0:T(8,128)(2,1)S(1)}, u32[]{:S(2)}, u32[]{:S(2)}) collective-permute-start(bf16[128,512]{1,0:T(8,128)(2,1)S(1)} %slice.8), channel_id=1, source_target_pairs={{0,16},{8,24},{16,0},{24,8},{1,17},{9,25},{17,1},{25,9},{2,18},{10... | collective-permute-start | bytes 393224 | tf_op jit(solution)/shard_map/ppermute | solution.py:20
  41.4 0.8 copy-start.1
  42.2 47.6 %copy-start.5 = (s32[512]{0:T(512)S(1)}, s32[512]{0:T(512)}, u32[]{:S(2)}) copy-start(s32[512]{0:T(512)} %param.10) | copy-start | bytes 6148
  61.1 1.4 copy-start.2
  65.1 24.1 %collective-permute-start.6 = (bf16[256,2048]{1,0:T(8,128)(2,1)}, bf16[256,2048]{1,0:T(8,128)(2,1)S(1)}, u32[]{:S(2)}, u32[]{:S(2)}) collective-permute-start(bf16[256,2048]{1,0:T(8,128)(2,1)} %get-tuple-element.7), channel_id=1, source_target_pairs={{0,2},{2,4},{4,6},{6,0},{1,3},{3,5},{5,7},{7,1},{8,10},{10,12},{12... | collective-permute-start | bytes 3145736 | tf_op jit(solution)/shard_map/ppermute | solution.py:20
  65.1 24.1 %collective-permute-start.7 = (bf16[256,2048]{1,0:T(8,128)(2,1)}, bf16[256,2048]{1,0:T(8,128)(2,1)S(1)}, u32[]{:S(2)}, u32[]{:S(2)}) collective-permute-start(bf16[256,2048]{1,0:T(8,128)(2,1)} %get-tuple-element.8), channel_id=1, source_target_pairs={{0,6},{2,0},{4,2},{6,4},{1,7},{3,1},{5,3},{7,5},{8,14},{10,8},{12,... | collective-permute-start | bytes 3145736 | tf_op jit(solution)/shard_map/ppermute | solution.py:20
  67.2 26.4 %collective-permute-start.10 = (bf16[512,2048]{1,0:T(8,128)(2,1)}, bf16[512,2048]{1,0:T(8,128)(2,1)}, u32[]{:S(2)}, u32[]{:S(2)}) collective-permute-start(bf16[512,2048]{1,0:T(8,128)(2,1)} %collective-permute-done.5.down_ref.refs_2_), channel_id=1, source_target_pairs={{0,1},{1,0},{2,3},{3,2},{4,5},{5,4},{6,7},{7,6},{8,9},{9,8},{10,11... | collective-permute-start | bytes 6291464 | tf_op jit(solution)/shard_map/ppermute | solution.py:20
  67.2 26.4 %collective-permute-start.9 = (bf16[512,2048]{1,0:T(8,128)(2,1)}, bf16[512,2048]{1,0:T(8,128)(2,1)}, u32[]{:S(2)}, u32[]{:S(2)}) collective-permute-start(bf16[512,2048]{1,0:T(8,128)(2,1)} %copy-done.2), channel_id=1, source_target_pairs={{0,1},{1,0},{2,3},{3,2},{4,5},{5,4},{6,7},{7,6},{8,9},{9,8},{10,11... | collective-permute-start | bytes 6291464 | tf_op jit(solution)/shard_map/ppermute | solution.py:20
  89.3 4.1 %collective-permute-start.11 = (bf16[256,2048]{1,0:T(8,128)(2,1)S(1)}, bf16[256,2048]{1,0:T(8,128)(2,1)S(1)}, u32[]{:S(2)}, u32[]{:S(2)}) collective-permute-start(bf16[256,2048]{1,0:T(8,128)(2,1)S(1)} %collective-permute-done.6.refs_3_), channel_id=1, source_target_pairs={{0,1},{1,0},{2,3},{3,2},{4,5},{5,4},{6,7},{7,6},{8,9},{9,8},{10,11... | collective-permute-start | bytes 3145736 | tf_op jit(solution)/shard_map/ppermute | solution.py:20
  89.3 4.3 %collective-permute-start.12 = (bf16[256,2048]{1,0:T(8,128)(2,1)S(1)}, bf16[256,2048]{1,0:T(8,128)(2,1)}, u32[]{:S(2)}, u32[]{:S(2)}) collective-permute-start(bf16[256,2048]{1,0:T(8,128)(2,1)S(1)} %collective-permute-done.7.refs_4_), channel_id=1, source_target_pairs={{0,1},{1,0},{2,3},{3,2},{4,5},{5,4},{6,7},{7,6},{8,9},{9,8},{10,11... | collective-permute-start | bytes 3145736 | tf_op jit(solution)/shard_map/ppermute | solution.py:20
  100.9 1.0 copy-start
  144.4 14.8 %all-to-all-start.1 = ((bf16[32,16,128]{2,1,0:T(8,128)(2,1)}), bf16[32,16,128]{2,1,0:T(8,128)(2,1)S(1)}, u32[]{:S(2)}, u32[]{:S(2)}) async-start(bf16[32,16,128]{2,1,0:T(8,128)(2,1)} %merge.1), calls=%async_computation.1 | async-start | bytes 262144 | tf_op jit(solution)/shard_map/all_to_all | solution.py:262
  159.2 0.6 copy-start.4
Sparse Core Ops, SparseCore 0:
  42.3 58.5 all-gather.1

commit v4 on v3

--- a/solution.py
+++ b/solution.py
@@ -9,7 +9,7 @@
 
 TILE = 512
 FA = 1 << 20
-SLICE = 1 << 36
+SLICE = 1 << 33
 BLOCK = 1 << 20
 F32 = jnp.float32
 BF16 = jnp.bfloat16
@@ -42,6 +42,34 @@
         got = block if by == 0 else shift(block, "x", by)
         out = lax.dynamic_update_slice(out, got, (((x - by) % 4) * 128, 0))
     return out
+
+
+def ring_z(block, before_third):
+    half = block.shape[0] // 2
+    right, left = [block], [block]
+    for step in range(3):
+        sent = (right[-1], left[-1])
+        if step == 2:
+            sent, before_third = lax.optimization_barrier((sent, before_third))
+        right.append(shift(sent[0], "z", 1))
+        left.append(shift(sent[1], "z", -1))
+    far = [shift(right[-1][:half], "z", 1), shift(left[-1][half:], "z", -1)]
+    return right + far + left[:0:-1], before_third
+
+
+def load_hidden(block_refs, hid_ref, sems):
+    half = hid_ref.shape[1] // 2
+    places = [hid_ref.at[i] for i in range(4)]
+    places += [hid_ref.at[4, pl.ds(0, half)], hid_ref.at[4, pl.ds(half, half)]]
+    places += [hid_ref.at[i] for i in range(5, 8)]
+    copies = [
+        pltpu.make_async_copy(ref, place, sems.at[i])
+        for i, (ref, place) in enumerate(zip(block_refs, places))
+    ]
+    for copy in copies:
+        copy.start()
+    for copy in copies:
+        copy.wait()
 
 
 def block_kernel(x_ref, hidden_ref, proj_in_ref, out_ref):
@@ -98,12 +126,14 @@
     return acc
 
 
-def head_kernel(pieces, slot_ref, hid_ref, proj_ref, tgt_ref, rows_ref, *refs):
-    heads, (out_ref, max_ref, rest_ref, hit_ref, sum_ref) = refs[: len(pieces)], refs[len(pieces) :]
+def head_kernel(pieces, slot_ref, *refs):
+    blocks, (proj_ref, tgt_ref, rows_ref), heads = refs[:9], refs[9:12], refs[12 : 12 + len(pieces)]
+    out_ref, max_ref, rest_ref, hit_ref, sum_ref, hid_ref, sems = refs[12 + len(pieces) :]
     step = pl.program_id(0)
 
     @pl.when(step == 0)
     def _():
+        load_hidden(blocks, hid_ref, sems)
         max_ref[...] = jnp.full_like(max_ref, -jnp.inf)
         rest_ref[...] = jnp.zeros_like(rest_ref)
         hit_ref[...] = jnp.zeros_like(hit_ref)
@@ -138,15 +168,15 @@
         out_ref[:, 128:256] = jnp.where(term == 0, high, jnp.where(term == 1, middle, low)).astype(BF16)
 
 
-def project_kernel(hid_ref, out_ref, sum_ref):
-    @pl.when(pl.program_id(0) == 0)
-    def _():
-        sum_ref[...] = jnp.zeros_like(sum_ref)
-
-    sum_ref[...] += lax.dot_general(
-        hid_ref[0, 512:], hid_ref[0, :512], (((1,), (1,)), ((), ())), preferred_element_type=F32
-    )
-    out_ref[...] = sum_ref[...].astype(BF16)
+def project_kernel(*refs):
+    out_ref, hid_ref, sems = refs[9:]
+    load_hidden(refs[:9], hid_ref, sems)
+    total = jnp.zeros((32, 512), F32)
+    for i in range(8):
+        total = total + lax.dot_general(
+            hid_ref[i, 512:], hid_ref[i, :512], (((1,), (1,)), ((), ())), preferred_element_type=F32
+        )
+    out_ref[...] = total.astype(BF16)
 
 
 def merge_kernel(got_ref, out_ref):
@@ -180,7 +210,7 @@
         out_ref[e] = summed[16 * e : 16 * e + 4] / length
 
 
-PARAMS = dict(dimension_semantics=("arbitrary",), vmem_limit_bytes=48 << 20)
+PARAMS = dict(dimension_semantics=("arbitrary",), vmem_limit_bytes=60 << 20)
 
 
 def head_spec(ref):
@@ -196,10 +226,11 @@
     me = z * 4 + x
 
     up, down = shift(head, "y", 1), shift(head, "y", -1)
+    head_swapped = swap(head)
+    hidden_states, head_swapped = lax.optimization_barrier((hidden_states, head_swapped))
     block = exchange_corners(with_columns(hidden_states, proj_in, x))
     mine = lax.dynamic_update_slice(along_x(block[:128]), block[128:], (512, 0))
-    hid = lax.all_gather(mine, "z", axis=0, tiled=False)
-    far_a, far_b = halves(up, down, block)
+    hid, (far_a, far_b) = ring_z(mine, halves(up, down, block))
     far_a, far_b = shift(far_a, "y", 1), shift(far_b, "y", -1)
 
     local_target = targets[:, None] - me * 2048
@@ -211,10 +242,16 @@
 
     items = [(head, 0, 0, 512), (up, 1, 0, 512), (down, 2, 0, 512)]
     items += [(far_a, 3, 0, 256), (far_b, 3, 256, 256)]
-    refs = [i[0] for i in items] + [swap(i[0]) for i in items]
+    refs = [i[0] for i in items]
+    near_later, _ = lax.optimization_barrier((refs[1:3], hid[2]))
     pieces = [i[1:] for i in items] + [(i[1] + 4, i[2], i[3]) for i in items]
-    slots = jnp.stack([slot(dy, dc) for dc in (0, 1) for dy in (0, -1, 1, 2)]).astype(jnp.int32)
-
+    slots = jnp.stack([slot(dy, dc) for dc in (0, 1) for dy in (0, -1, 1, 2)])
+    slots = ((z - slots) % 8).astype(jnp.int32)
+
+    far_later, _, rows, local_target, slots = lax.optimization_barrier(
+        (refs[3:], (hid[4], hid[5]), rows, local_target, slots)
+    )
+    refs += [head_swapped] + [swap(r) for r in near_later + far_later]
     out = pl.pallas_call(
         functools.partial(head_kernel, pieces),
         out_shape=jax.ShapeDtypeStruct((512, 384), BF16),
@@ -222,33 +259,32 @@
             num_scalar_prefetch=1,
             grid=(2048 // TILE,),
             in_specs=[
-                whole((8, 544, 512)),
+                *[pl.BlockSpec(memory_space=pl.ANY)] * 9,
                 pl.BlockSpec((TILE, 128), lambda i, s: (i, 0)),
                 whole((512, 1)),
                 whole((512, 128)),
             ]
             + [head_spec(r) for r in refs],
             out_specs=whole((512, 384)),
-            scratch_shapes=[pltpu.VMEM((512, 1), F32)] * 3 + [pltpu.VMEM((512, 128), F32)],
+            scratch_shapes=[pltpu.VMEM((512, 1), F32)] * 3
+            + [pltpu.VMEM((512, 128), F32), pltpu.VMEM((8, 544, 512), BF16)]
+            + [pltpu.SemaphoreType.DMA((9,))],
         ),
         compiler_params=pltpu.CompilerParams(**PARAMS),
         cost_estimate=pl.CostEstimate(flops=FA, bytes_accessed=1 << 20, transcendentals=0),
         name="head",
-    )(slots, hid, proj_out, local_target, rows, *refs)
+    )(slots, *hid, proj_out, local_target, rows, *refs)
 
     got = lax.all_to_all(out, ("z", "x"), 0, 0, tiled=True).reshape(32, 16, 384)
     in_proj = pl.pallas_call(
         project_kernel,
         out_shape=jax.ShapeDtypeStruct((32, 512), BF16),
-        grid=(8,),
-        in_specs=[
-            pl.BlockSpec((1, 544, 512), lambda i: (i, 0, 0)),
-        ],
-        out_specs=pl.BlockSpec((32, 512), lambda i: (0, 0)),
-        scratch_shapes=[pltpu.VMEM((32, 512), F32)],
+        in_specs=[pl.BlockSpec(memory_space=pl.ANY)] * 9,
+        scratch_shapes=[pltpu.VMEM((8, 544, 512), BF16), pltpu.SemaphoreType.DMA((9,))],
+        compiler_params=pltpu.CompilerParams(vmem_limit_bytes=48 << 20),
         cost_estimate=pl.CostEstimate(flops=1 << 30, bytes_accessed=4 << 20, transcendentals=0),
         name="project",
-    )(hid)
+    )(*hid)
     in_proj = lax.dynamic_slice_in_dim(in_proj, 4 * z, 4, 0)
     in_proj = jnp.concatenate([in_proj, jnp.zeros((12, 512), BF16)], axis=0)
     in_vmem = pl.BlockSpec(memory_space=pltpu.VMEM)

time: 169 us -> 170 us (level)
  starting transfers between devices: 22 us -> 36.8 us
  between operations: 13.5 us -> 0.24 us
  waiting for transfers between devices: 70.6 us -> 62.2 us
  blocking collectives: 22.4 us -> 28.6 us
  local copies, waits for them, and re-layouts: 5.51 us -> 8.61 us
    ppermute x12 -> x20, starting transfers between devices: 11.7 us -> 27.4 us  [shift(): return lax.ppermute(x, axis, [(i, (i + by) % n) for i in range(n)])]
    all_gather x1 -> x0, waiting for transfers between devices: 7.37 us -> none  [local(): hid = lax.all_gather(mine, 'z', axis=0, tiled=False)]
    all_to_all x1, blocking collectives: 22.4 us -> 28.6 us  [local(): got = lax.all_to_all(out, ('z', 'x'), 0, 0, tiled=True).reshape(32, 16, 384)]
    pallas_call x1, Pallas kernels: 6.29 us -> 2.03 us  [local(): pl.pallas_call(project_kernel, out_shape=jax.ShapeDtypeStruct((32, 512),...]
    unnamed x12 -> x46, local copies, waits for them, and re-layouts: 3.85 us -> 6.92 us
    pallas_call x1, Pallas kernels: 18 us -> 20.8 us  [local(): pl.pallas_call(functools.partial(head_kernel, pieces), out_shape=jax.Shap...]
    ppermute x1, waiting for transfers between devices: 10.2 us -> 12.8 us  [exchange_corners(): return lax.ppermute(x, ('z', 'x', 'y', 'c'), pairs)]
    ppermute x12 -> x20, waiting for transfers between devices: 50.1 us -> 47.7 us  [shift(): return lax.ppermute(x, axis, [(i, (i + by) % n) for i in range(n)])]
  transfers between devices with their start and end apart: 15 -> 22, of which waited for: 9 -> 15; matrix products, arithmetic and copies ran while one was open for 2% -> 2% of each run, Pallas kernels for 6% -> 4%
where the time goes in v4:
time: 170 us
  waiting for transfers between devices  62.2 us (37%)
  starting transfers between devices  36.8 us (22%)
  Pallas kernels  31.2 us (18%)
  blocking collectives  28.6 us (17%)
  local copies, waits for them, and re-layouts  8.61 us (5%)
    ppermute x20, waiting for transfers between devices, shift(): return lax.ppermute(x, axis, [(i, (i + by) % n) for i in range(n)])  47.7 us
    all_to_all x1, blocking collectives, local(): got = lax.all_to_all(out, ('z', 'x'), 0, 0, tiled=True).reshape(32, 16, 384)  28.6 us
    ppermute x20, starting transfers between devices, shift(): return lax.ppermute(x, axis, [(i, (i + by) % n) for i in range(n)])  27.4 us
    pallas_call x1, Pallas kernels, local(): pl.pallas_call(functools.partial(head_kernel, pieces), out_shape=jax.Shap...  20.8 us
    ppermute x1, waiting for transfers between devices, exchange_corners(): return lax.ppermute(x, ('z', 'x', 'y', 'c'), pairs)  12.8 us
    unnamed x46, local copies, waits for them, and re-layouts  6.92 us
    ppermute x1, starting transfers between devices, exchange_corners(): return lax.ppermute(x, ('z', 'x', 'y', 'c'), pairs)  5.05 us
    all_to_all x1, starting transfers between devices, local(): lax.all_to_all(merged, ('z', 'x'), 0, 0, tiled=True).reshape(512, 128)  4.31 us
  transfers between devices with their start and end apart: 22, of which 15 were waited for; matrix products, arithmetic and copies ran while one was open for 2% of the time, Pallas kernels for 4%

profile of v4, /device:TPU:8, one launch (start us, length us, event | category | flops | bytes accessed | tf_op | source)
XLA Modules:
  0.0 169.7 jit_solution(11551920281201389985)
XLA Ops:
  0.0 2.2 %collective-permute-start.10 = (bf16[512,2048]{1,0:T(8,128)(2,1)}, bf16[512,2048]{1,0:T(8,128)(2,1)}, u32[]{:S(2)}, u32[]{:S(2)}) collective-permute-start(bf16[512,2048]{1,0:T(8,128)(2,1)} %refs_12_.1), channel_id=1, source_target_pairs={{0,6},{2,0},{4,2},{6,4},{1,7},{3,1},{5,3},{7,5},{8,14},{10,8},{12,... | collective-permute-start | bytes 6291464 | tf_op jit(solution)/shard_map/ppermute | solution.py:20
  2.2 2.2 %collective-permute-done.refs_17_ = bf16[512,2048]{1,0:T(8,128)(2,1)S(1)} collective-permute-done((bf16[512,2048]{1,0:T(8,128)(2,1)}, bf16[512,2048]{1,0:T(8,128)(2,1)S(1)}, u32[]{:S(2)}, u32[]{:S(2)}) %collective-permute-start) | collective-permute-done | bytes 2097184 | tf_op jit(solution)/shard_map/ppermute | solution.py:20
  4.4 2.1 %block.1 = bf16[160,512]{1,0:T(8,128)(2,1)} custom-call(s32[1]{0:T(128)} %bitcast.x_ref, bf16[128,512]{1,0:T(8,128)(2,1)} %hidden_ref, bf16[512,128]{1,0:T(8,128)(2,1)} %proj_in_ref.1), custom_call_target="tpu_custom_call" | custom-call | flops 1048576 | bytes 1048576 | tf_op jit(solution)/shard_map/block/pallas_call | solution.py:86
  6.4 5.1 %collective-permute-start.1 = (bf16[160,512]{1,0:T(8,128)(2,1)}, bf16[160,512]{1,0:T(8,128)(2,1)S(1)}, u32[]{:S(2)}, u32[]{:S(2)}) collective-permute-start(bf16[160,512]{1,0:T(8,128)(2,1)} %block.1), channel_id=1, source_target_pairs={{0,0},{1,32},{2,64},{3,96},{4,128},{5,160},{6,192},{7,224},{8,8},{... | collective-permute-start | bytes 491528 | tf_op jit(solution)/shard_map/ppermute | solution.py:35
  11.5 12.8 %collective-permute-done.1.early_ref = bf16[160,512]{1,0:T(8,128)(2,1)S(1)} collective-permute-done((bf16[160,512]{1,0:T(8,128)(2,1)}, bf16[160,512]{1,0:T(8,128)(2,1)S(1)}, u32[]{:S(2)}, u32[]{:S(2)}) %collective-permute-start.1) | collective-permute-done | bytes 163872 | tf_op jit(solution)/shard_map/ppermute | solution.py:35
  24.4 1.6 collective-permute-start.2
  26.0 1.7 %collective-permute-start.3 = (bf16[128,512]{1,0:T(8,128)(2,1)S(1)}, bf16[128,512]{1,0:T(8,128)(2,1)S(1)}, u32[]{:S(2)}, u32[]{:S(2)}) collective-permute-start(bf16[128,512]{1,0:T(8,128)(2,1)S(1)} %get-tuple-element.35), channel_id=1, source_target_pairs={{0,24},{8,0},{16,8},{24,16},{1,25},{9,1},{17,9},{25,17},{2,26},{10... | collective-permute-start | bytes 393224 | tf_op jit(solution)/shard_map/ppermute | solution.py:20
  27.7 1.8 %collective-permute-start.4 = (bf16[128,512]{1,0:T(8,128)(2,1)S(1)}, bf16[128,512]{1,0:T(8,128)(2,1)S(1)}, u32[]{:S(2)}, u32[]{:S(2)}) collective-permute-start(bf16[128,512]{1,0:T(8,128)(2,1)S(1)} %get-tuple-element.35), channel_id=1, source_target_pairs={{0,16},{8,24},{16,0},{24,8},{1,17},{9,25},{17,1},{25,9},{2,18},{10... | collective-permute-start | bytes 393224 | tf_op jit(solution)/shard_map/ppermute | solution.py:20
  30.9 3.2 %collective-permute-done.4 = bf16[128,512]{1,0:T(8,128)(2,1)S(1)} collective-permute-done((bf16[128,512]{1,0:T(8,128)(2,1)S(1)}, bf16[128,512]{1,0:T(8,128)(2,1)S(1)}, u32[]{:S(2)}, u32[]{:S(2)}) %collective-permute-start.4) | collective-permute-done | bytes 131104 | tf_op jit(solution)/shard_map/ppermute | solution.py:20
  35.0 2.5 %collective-permute-start.7 = (bf16[544,512]{1,0:T(8,128)(2,1)S(1)}, bf16[544,512]{1,0:T(8,128)(2,1)S(1)}, u32[]{:S(2)}, u32[]{:S(2)}) collective-permute-start(bf16[544,512]{1,0:T(8,128)(2,1)S(1)} %slice_dynamic-update-slice_fusion.refs_0_), channel_id=1, source_target_pairs={{0,224},{32,0},{64,32},{96,64},{128,96},{160,128},{192,160},{224,1... | collective-permute-start | bytes 1671176 | tf_op jit(solution)/shard_map/ppermute | solution.py:20
  37.6 10.4 %collective-permute-done.5.refs_1_ = bf16[544,512]{1,0:T(8,128)(2,1)S(1)} collective-permute-done((bf16[544,512]{1,0:T(8,128)(2,1)S(1)}, bf16[544,512]{1,0:T(8,128)(2,1)S(1)}, u32[]{:S(2)}, u32[]{:S(2)}) %collective-permute-start.5) | collective-permute-done | bytes 557088 | tf_op jit(solution)/shard_map/ppermute | solution.py:20
  48.4 2.8 %collective-permute-start.8 = (bf16[544,512]{1,0:T(8,128)(2,1)S(1)}, bf16[544,512]{1,0:T(8,128)(2,1)S(1)}, u32[]{:S(2)}, u32[]{:S(2)}) collective-permute-start(bf16[544,512]{1,0:T(8,128)(2,1)S(1)} %collective-permute-done.7.refs_8_), channel_id=1, source_target_pairs={{0,224},{32,0},{64,32},{96,64},{128,96},{160,128},{192,160},{224,1... | collective-permute-start | bytes 1671176 | tf_op jit(solution)/shard_map/ppermute | solution.py:20
  51.2 6.0 %collective-permute-done.9.up_ref.refs_13_ = bf16[512,2048]{1,0:T(8,128)(2,1)} collective-permute-done((bf16[512,2048]{1,0:T(8,128)(2,1)}, bf16[512,2048]{1,0:T(8,128)(2,1)}, u32[]{:S(2)}, u32[]{:S(2)}) %collective-permute-start.9) | collective-permute-done | bytes 2097184 | tf_op jit(solution)/shard_map/ppermute | solution.py:20
  57.3 2.6 %halves.1 = (bf16[256,2048]{1,0:T(8,128)(2,1)}, bf16[256,2048]{1,0:T(8,128)(2,1)}) custom-call(bf16[512,2048]{1,0:T(8,128)(2,1)} %collective-permute-done.9.up_ref.refs_13_, bf16[512,2048]{1,0:T(8,128)(2,1)} %collective-permute-done.10.down_ref.refs_14_, bf16[160,512]{1,0:T(8,128)(2,1)} %copy-done.21), custom_call_target="tpu_custom_call" | custom-call | flops 8589934592 | bytes 4194304 | tf_op jit(solution)/shard_map/halves/pallas_call | solution.py:104
  59.9 2.0 %collective-permute-done.6.refs_2_ = bf16[544,512]{1,0:T(8,128)(2,1)S(1)} collective-permute-done((bf16[544,512]{1,0:T(8,128)(2,1)S(1)}, bf16[544,512]{1,0:T(8,128)(2,1)S(1)}, u32[]{:S(2)}, u32[]{:S(2)}) %collective-permute-start.6) | collective-permute-done | bytes 557088 | tf_op jit(solution)/shard_map/ppermute | solution.py:20
  61.9 5.4 %collective-permute-start.11 = (bf16[544,512]{1,0:T(8,128)(2,1)S(1)}, bf16[544,512]{1,0:T(8,128)(2,1)S(1)}, u32[]{:S(2)}, u32[]{:S(2)}) collective-permute-start(bf16[544,512]{1,0:T(8,128)(2,1)S(1)} %collective-permute-done.6.refs_2_), channel_id=1, source_target_pairs={{0,32},{32,64},{64,96},{96,128},{128,160},{160,192},{192,224},{224... | collective-permute-start | bytes 1671176 | tf_op jit(solution)/shard_map/ppermute | solution.py:20
  67.4 4.3 %collective-permute-start.15 = (bf16[256,2048]{1,0:T(8,128)(2,1)}, bf16[256,2048]{1,0:T(8,128)(2,1)}, u32[]{:S(2)}, u32[]{:S(2)}) collective-permute-start(bf16[256,2048]{1,0:T(8,128)(2,1)} %get-tuple-element.25), channel_id=1, source_target_pairs={{0,2},{2,4},{4,6},{6,0},{1,3},{3,5},{5,7},{7,1},{8,10},{10,12},{12... | collective-permute-start | bytes 3145736 | tf_op jit(solution)/shard_map/ppermute | solution.py:20
  71.6 7.6 %collective-permute-done.11.refs_3_ = bf16[544,512]{1,0:T(8,128)(2,1)S(1)} collective-permute-done((bf16[544,512]{1,0:T(8,128)(2,1)S(1)}, bf16[544,512]{1,0:T(8,128)(2,1)S(1)}, u32[]{:S(2)}, u32[]{:S(2)}) %collective-permute-start.11) | collective-permute-done | bytes 557088 | tf_op jit(solution)/shard_map/ppermute | solution.py:20
  79.2 1.9 %collective-permute-done.13.refs_6_ = bf16[544,512]{1,0:T(8,128)(2,1)S(1)} collective-permute-done((bf16[544,512]{1,0:T(8,128)(2,1)S(1)}, bf16[544,512]{1,0:T(8,128)(2,1)S(1)}, u32[]{:S(2)}, u32[]{:S(2)}) %collective-permute-start.13) | collective-permute-done | bytes 557088 | tf_op jit(solution)/shard_map/ppermute | solution.py:20
  81.1 2.7 %collective-permute-start.12 = (bf16[272,512]{1,0:T(8,128)(2,1)S(1)}, bf16[272,512]{1,0:T(8,128)(2,1)S(1)}, u32[]{:S(2)}, u32[]{:S(2)}) collective-permute-start(bf16[272,512]{1,0:T(8,128)(2,1)S(1)} %slice.18), channel_id=1, source_target_pairs={{0,32},{32,64},{64,96},{96,128},{128,160},{160,192},{192,224},{224... | collective-permute-start | bytes 835592 | tf_op jit(solution)/shard_map/ppermute | solution.py:20
  83.9 5.8 %collective-permute-done.12.refs_4_ = bf16[272,512]{1,0:T(8,128)(2,1)S(1)} collective-permute-done((bf16[272,512]{1,0:T(8,128)(2,1)S(1)}, bf16[272,512]{1,0:T(8,128)(2,1)S(1)}, u32[]{:S(2)}, u32[]{:S(2)}) %collective-permute-start.12) | collective-permute-done | bytes 278560 | tf_op jit(solution)/shard_map/ppermute | solution.py:20
  90.8 1.5 fusion.2.refs_11_
  92.3 4.0 %collective-permute-done.14.refs_5_ = bf16[272,512]{1,0:T(8,128)(2,1)S(1)} collective-permute-done((bf16[272,512]{1,0:T(8,128)(2,1)S(1)}, bf16[272,512]{1,0:T(8,128)(2,1)S(1)}, u32[]{:S(2)}, u32[]{:S(2)}) %collective-permute-start.14) | collective-permute-done | bytes 278560 | tf_op jit(solution)/shard_map/ppermute | solution.py:20
  97.9 1.5 collective-permute-done.19.refs_20_
  99.4 1.5 collective-permute-done.20.refs_21_
  100.9 20.8 %head.1 = bf16[512,384]{1,0:T(8,128)(2,1)} custom-call(s32[8]{0:T(128)} %and_select_fusion.slot_ref, bf16[544,512]{1,0:T(8,128)(2,1)} %copy-done, bf16[544,512]{1,0:T(8,128)(2,1)} %copy-done.6, bf16[544,512]{1,0:T(8,128)(2,1)} %copy-done.10, bf16[544,512]{1,0:T(8,128)(2,1)} %copy-done.2, bf16[272,512]{1,0:T(8,128)(2,1)} %copy-done.14, ...), custom_call_target="tpu_custom_call" | custom-call | flops 1048576 | bytes 1048576 | tf_op jit(solution)/shard_map/head/pallas_call | solution.py:255
  121.8 28.6 %all_to_all.14.got_ref = bf16[32,16,384]{2,1,0:T(8,128)(2,1)} all-to-all(bf16[32,16,384]{2,1,0:T(8,128)(2,1)} %bitcast.13), channel_id=1, replica_groups=mesh['z'=8,'x'=4,'y'=4,'c'=2] {'z','x'}, dimensions={0} | all-to-all | bytes 786432 | tf_op jit(solution)/shard_map/all_to_all | solution.py:278
  150.4 2.0 %merge.1 = bf16[32,16,128]{2,1,0:T(8,128)(2,1)} custom-call(bf16[32,16,384]{2,1,0:T(8,128)(2,1)} %all_to_all.14.got_ref), custom_call_target="tpu_custom_call" | custom-call | tf_op jit(solution)/shard_map/merge/pallas_call | solution.py:291
  152.4 4.3 %all-to-all-start.1 = ((bf16[32,16,128]{2,1,0:T(8,128)(2,1)}), bf16[32,16,128]{2,1,0:T(8,128)(2,1)S(1)}, u32[]{:S(2)}, u32[]{:S(2)}) async-start(bf16[32,16,128]{2,1,0:T(8,128)(2,1)} %merge.1), calls=%async_computation.1 | async-start | bytes 262144 | tf_op jit(solution)/shard_map/all_to_all | solution.py:298
  162.9 2.0 %project.1 = bf16[32,512]{1,0:T(8,128)(2,1)S(1)} custom-call(bf16[544,512]{1,0:T(8,128)(2,1)S(1)} %copy-done.1, bf16[544,512]{1,0:T(8,128)(2,1)S(1)} %copy-done.7, bf16[544,512]{1,0:T(8,128)(2,1)S(1)} %copy-done.11, bf16[544,512]{1,0:T(8,128)(2,1)S(1)} %copy-done.3, bf16[272,512]{1,0:T(8,128)(2,1)S(1)} %copy-done.15, bf16[272,512]{1,0:T(8,128)(2,1)S(1)} %copy-done.17, ...), custom_call_target="tpu_custom_call" | custom-call | flops 1073741824 | bytes 4194304 | tf_op jit(solution)/shard_map/project/pallas_call | solution.py:279
  165.6 1.7 %all-to-all-done.1 = bf16[32,16,128]{2,1,0:T(8,128)(2,1)S(1)} async-done(((bf16[32,16,128]{2,1,0:T(8,128)(2,1)}), bf16[32,16,128]{2,1,0:T(8,128)(2,1)S(1)}, u32[]{:S(2)}, u32[]{:S(2)}) %all-to-all-start.1) | async-done | bytes 131104 | tf_op jit(solution)/shard_map/all_to_all | solution.py:298
  167.9 1.7 %final.1 = f32[8,4,128]{2,1,0:T(4,128)} custom-call(s32[1,8]{1,0:T(1,128)} %lengths_ref.1, bf16[16,512]{1,0:T(8,128)(2,1)} %concatenate.3.in_ref, bf16[512,128]{1,0:T(8,128)(2,1)} %bitcast.14), custom_call_target="tpu_custom_call" | custom-call | tf_op jit(solution)/shard_map/final/pallas_call | solution.py:299
  (80 shorter events, 12.9 us)
Async XLA Ops:
  0.0 4.4 %collective-permute-start = (bf16[512,2048]{1,0:T(8,128)(2,1)}, bf16[512,2048]{1,0:T(8,128)(2,1)S(1)}, u32[]{:S(2)}, u32[]{:S(2)}) collective-permute-start(bf16[512,2048]{1,0:T(8,128)(2,1)} %refs_12_.1), channel_id=1, source_target_pairs={{0,1},{1,0},{2,3},{3,2},{4,5},{5,4},{6,7},{7,6},{8,9},{9,8},{10,11... | collective-permute-start | bytes 6291464 | tf_op jit(solution)/shard_map/ppermute | solution.py:20
  0.0 51.2 %collective-permute-start.10 = (bf16[512,2048]{1,0:T(8,128)(2,1)}, bf16[512,2048]{1,0:T(8,128)(2,1)}, u32[]{:S(2)}, u32[]{:S(2)}) collective-permute-start(bf16[512,2048]{1,0:T(8,128)(2,1)} %refs_12_.1), channel_id=1, source_target_pairs={{0,6},{2,0},{4,2},{6,4},{1,7},{3,1},{5,3},{7,5},{8,14},{10,8},{12,... | collective-permute-start | bytes 6291464 | tf_op jit(solution)/shard_map/ppermute | solution.py:20
  2.2 55.1 %collective-permute-start.9 = (bf16[512,2048]{1,0:T(8,128)(2,1)}, bf16[512,2048]{1,0:T(8,128)(2,1)}, u32[]{:S(2)}, u32[]{:S(2)}) collective-permute-start(bf16[512,2048]{1,0:T(8,128)(2,1)} %refs_12_.1), channel_id=1, source_target_pairs={{0,2},{2,4},{4,6},{6,0},{1,3},{3,5},{5,7},{7,1},{8,10},{10,12},{12... | collective-permute-start | bytes 6291464 | tf_op jit(solution)/shard_map/ppermute | solution.py:20
  6.4 17.9 %collective-permute-start.1 = (bf16[160,512]{1,0:T(8,128)(2,1)}, bf16[160,512]{1,0:T(8,128)(2,1)S(1)}, u32[]{:S(2)}, u32[]{:S(2)}) collective-permute-start(bf16[160,512]{1,0:T(8,128)(2,1)} %block.1), channel_id=1, source_target_pairs={{0,0},{1,32},{2,64},{3,96},{4,128},{5,160},{6,192},{7,224},{8,8},{... | collective-permute-start | bytes 491528 | tf_op jit(solution)/shard_map/ppermute | solution.py:35
  24.3 33.0 %copy-start.21 = (bf16[160,512]{1,0:T(8,128)(2,1)}, bf16[160,512]{1,0:T(8,128)(2,1)S(1)}, u32[]{:S(2)}) copy-start(bf16[160,512]{1,0:T(8,128)(2,1)S(1)} %collective-permute-done.1.early_ref) | copy-start | bytes 491524
  24.4 6.3 %collective-permute-start.2 = (bf16[128,512]{1,0:T(8,128)(2,1)S(1)}, bf16[128,512]{1,0:T(8,128)(2,1)S(1)}, u32[]{:S(2)}, u32[]{:S(2)}) collective-permute-start(bf16[128,512]{1,0:T(8,128)(2,1)S(1)} %get-tuple-element.35), channel_id=1, source_target_pairs={{0,8},{8,16},{16,24},{24,0},{1,9},{9,17},{17,25},{25,1},{2,10},{10... | collective-permute-start | bytes 393224 | tf_op jit(solution)/shard_map/ppermute | solution.py:20
  26.0 5.0 %collective-permute-start.3 = (bf16[128,512]{1,0:T(8,128)(2,1)S(1)}, bf16[128,512]{1,0:T(8,128)(2,1)S(1)}, u32[]{:S(2)}, u32[]{:S(2)}) collective-permute-start(bf16[128,512]{1,0:T(8,128)(2,1)S(1)} %get-tuple-element.35), channel_id=1, source_target_pairs={{0,24},{8,0},{16,8},{24,16},{1,25},{9,1},{17,9},{25,17},{2,26},{10... | collective-permute-start | bytes 393224 | tf_op jit(solution)/shard_map/ppermute | solution.py:20
  27.7 6.5 %collective-permute-start.4 = (bf16[128,512]{1,0:T(8,128)(2,1)S(1)}, bf16[128,512]{1,0:T(8,128)(2,1)S(1)}, u32[]{:S(2)}, u32[]{:S(2)}) collective-permute-start(bf16[128,512]{1,0:T(8,128)(2,1)S(1)} %get-tuple-element.35), channel_id=1, source_target_pairs={{0,16},{8,24},{16,0},{24,8},{1,17},{9,25},{17,1},{25,9},{2,18},{10... | collective-permute-start | bytes 393224 | tf_op jit(solution)/shard_map/ppermute | solution.py:20
  34.2 25.7 %copy-start = (bf16[544,512]{1,0:T(8,128)(2,1)}, bf16[544,512]{1,0:T(8,128)(2,1)S(1)}, u32[]{:S(2)}) copy-start(bf16[544,512]{1,0:T(8,128)(2,1)S(1)} %slice_dynamic-update-slice_fusion.refs_0_) | copy-start | bytes 1671172
  34.2 49.7 %copy-start.22 = (s32[512]{0:T(512)S(1)}, s32[512]{0:T(512)}, u32[]{:S(2)}) copy-start(s32[512]{0:T(512)} %param.10) | copy-start | bytes 6148
  34.2 56.6 %copy-start.19 = (bf16[2048,128]{1,0:T(8,128)(2,1)S(1)}, bf16[2048,128]{1,0:T(8,128)(2,1)}, u32[]{:S(2)}) copy-start(bf16[2048,128]{1,0:T(8,128)(2,1)} %refs_9_.1) | copy-start | bytes 1572868
  34.2 13.7 %collective-permute-start.5 = (bf16[544,512]{1,0:T(8,128)(2,1)S(1)}, bf16[544,512]{1,0:T(8,128)(2,1)S(1)}, u32[]{:S(2)}, u32[]{:S(2)}) collective-permute-start(bf16[544,512]{1,0:T(8,128)(2,1)S(1)} %slice_dynamic-update-slice_fusion.refs_0_), channel_id=1, source_target_pairs={{0,32},{32,64},{64,96},{96,128},{128,160},{160,192},{192,224},{224... | collective-permute-start | bytes 1671176 | tf_op jit(solution)/shard_map/ppermute | solution.py:20
  35.0 13.4 %collective-permute-start.7 = (bf16[544,512]{1,0:T(8,128)(2,1)S(1)}, bf16[544,512]{1,0:T(8,128)(2,1)S(1)}, u32[]{:S(2)}, u32[]{:S(2)}) collective-permute-start(bf16[544,512]{1,0:T(8,128)(2,1)S(1)} %slice_dynamic-update-slice_fusion.refs_0_), channel_id=1, source_target_pairs={{0,224},{32,0},{64,32},{96,64},{128,96},{160,128},{192,160},{224,1... | collective-permute-start | bytes 1671176 | tf_op jit(solution)/shard_map/ppermute | solution.py:20
  48.0 13.9 %collective-permute-start.6 = (bf16[544,512]{1,0:T(8,128)(2,1)S(1)}, bf16[544,512]{1,0:T(8,128)(2,1)S(1)}, u32[]{:S(2)}, u32[]{:S(2)}) collective-permute-start(bf16[544,512]{1,0:T(8,128)(2,1)S(1)} %collective-permute-done.5.refs_1_), channel_id=1, source_target_pairs={{0,32},{32,64},{64,96},{96,128},{128,160},{160,192},{192,224},{224... | collective-permute-start | bytes 1671176 | tf_op jit(solution)/shard_map/ppermute | solution.py:20
  48.4 13.5 %collective-permute-start.8 = (bf16[544,512]{1,0:T(8,128)(2,1)S(1)}, bf16[544,512]{1,0:T(8,128)(2,1)S(1)}, u32[]{:S(2)}, u32[]{:S(2)}) collective-permute-start(bf16[544,512]{1,0:T(8,128)(2,1)S(1)} %collective-permute-done.7.refs_8_), channel_id=1, source_target_pairs={{0,224},{32,0},{64,32},{96,64},{128,96},{160,128},{192,160},{224,1... | collective-permute-start | bytes 1671176 | tf_op jit(solution)/shard_map/ppermute | solution.py:20
  61.9 39.0 %copy-start.10 = (bf16[544,512]{1,0:T(8,128)(2,1)}, bf16[544,512]{1,0:T(8,128)(2,1)S(1)}, u32[]{:S(2)}) copy-start(bf16[544,512]{1,0:T(8,128)(2,1)S(1)} %collective-permute-done.6.refs_2_) | copy-start | bytes 1671172
  61.9 35.1 %copy-start.12 = (bf16[544,512]{1,0:T(8,128)(2,1)}, bf16[544,512]{1,0:T(8,128)(2,1)S(1)}, u32[]{:S(2)}) copy-start(bf16[544,512]{1,0:T(8,128)(2,1)S(1)} %collective-permute-done.8.refs_7_) | copy-start | bytes 1671172
  61.9 17.3 %collective-permute-start.11 = (bf16[544,512]{1,0:T(8,128)(2,1)S(1)}, bf16[544,512]{1,0:T(8,128)(2,1)S(1)}, u32[]{:S(2)}, u32[]{:S(2)}) collective-permute-start(bf16[544,512]{1,0:T(8,128)(2,1)S(1)} %collective-permute-done.6.refs_2_), channel_id=1, source_target_pairs={{0,32},{32,64},{64,96},{96,128},{128,160},{160,192},{192,224},{224... | collective-permute-start | bytes 1671176 | tf_op jit(solution)/shard_map/ppermute | solution.py:20
  67.3 13.8 %collective-permute-start.13 = (bf16[544,512]{1,0:T(8,128)(2,1)S(1)}, bf16[544,512]{1,0:T(8,128)(2,1)S(1)}, u32[]{:S(2)}, u32[]{:S(2)}) collective-permute-start(bf16[544,512]{1,0:T(8,128)(2,1)S(1)} %collective-permute-done.8.refs_7_), channel_id=1, source_target_pairs={{0,224},{32,0},{64,32},{96,64},{128,96},{160,128},{192,160},{224,1... | collective-permute-start | bytes 1671176 | tf_op jit(solution)/shard_map/ppermute | solution.py:20
  67.4 29.0 %collective-permute-start.15 = (bf16[256,2048]{1,0:T(8,128)(2,1)}, bf16[256,2048]{1,0:T(8,128)(2,1)}, u32[]{:S(2)}, u32[]{:S(2)}) collective-permute-start(bf16[256,2048]{1,0:T(8,128)(2,1)} %get-tuple-element.25), channel_id=1, source_target_pairs={{0,2},{2,4},{4,6},{6,0},{1,3},{3,5},{5,7},{7,1},{8,10},{10,12},{12... | collective-permute-start | bytes 3145736 | tf_op jit(solution)/shard_map/ppermute | solution.py:20
  71.6 24.7 %collective-permute-start.16 = (bf16[256,2048]{1,0:T(8,128)(2,1)}, bf16[256,2048]{1,0:T(8,128)(2,1)}, u32[]{:S(2)}, u32[]{:S(2)}) collective-permute-start(bf16[256,2048]{1,0:T(8,128)(2,1)} %get-tuple-element.26), channel_id=1, source_target_pairs={{0,6},{2,0},{4,2},{6,4},{1,7},{3,1},{5,3},{7,5},{8,14},{10,8},{12,... | collective-permute-start | bytes 3145736 | tf_op jit(solution)/shard_map/ppermute | solution.py:20
  71.6 26.3 %collective-permute-start.17 = (bf16[512,2048]{1,0:T(8,128)(2,1)}, bf16[512,2048]{1,0:T(8,128)(2,1)}, u32[]{:S(2)}, u32[]{:S(2)}) collective-permute-start(bf16[512,2048]{1,0:T(8,128)(2,1)} %collective-permute-done.9.up_ref.refs_13_), channel_id=1, source_target_pairs={{0,1},{1,0},{2,3},{3,2},{4,5},{5,4},{6,7},{7,6},{8,9},{9,8},{10,11... | collective-permute-start | bytes 6291464 | tf_op jit(solution)/shard_map/ppermute | solution.py:20
  79.2 21.7 %copy-start.2 = (bf16[544,512]{1,0:T(8,128)(2,1)}, bf16[544,512]{1,0:T(8,128)(2,1)S(1)}, u32[]{:S(2)}) copy-start(bf16[544,512]{1,0:T(8,128)(2,1)S(1)} %collective-permute-done.11.refs_3_) | copy-start | bytes 1671172
  79.2 18.7 %collective-permute-start.18 = (bf16[512,2048]{1,0:T(8,128)(2,1)}, bf16[512,2048]{1,0:T(8,128)(2,1)}, u32[]{:S(2)}, u32[]{:S(2)}) collective-permute-start(bf16[512,2048]{1,0:T(8,128)(2,1)} %collective-permute-done.10.down_ref.refs_14_), channel_id=1, source_target_pairs={{0,1},{1,0},{2,3},{3,2},{4,5},{5,4},{6,7},{7,6},{8,9},{9,8},{10,11... | collective-permute-start | bytes 6291464 | tf_op jit(solution)/shard_map/ppermute | solution.py:20
  81.1 8.6 %collective-permute-start.12 = (bf16[272,512]{1,0:T(8,128)(2,1)S(1)}, bf16[272,512]{1,0:T(8,128)(2,1)S(1)}, u32[]{:S(2)}, u32[]{:S(2)}) collective-permute-start(bf16[272,512]{1,0:T(8,128)(2,1)S(1)} %slice.18), channel_id=1, source_target_pairs={{0,32},{32,64},{64,96},{96,128},{128,160},{160,192},{192,224},{224... | collective-permute-start | bytes 835592 | tf_op jit(solution)/shard_map/ppermute | solution.py:20
  89.8 6.5 %collective-permute-start.14 = (bf16[272,512]{1,0:T(8,128)(2,1)S(1)}, bf16[272,512]{1,0:T(8,128)(2,1)S(1)}, u32[]{:S(2)}, u32[]{:S(2)}) collective-permute-start(bf16[272,512]{1,0:T(8,128)(2,1)S(1)} %slice.19), channel_id=1, source_target_pairs={{0,224},{32,0},{64,32},{96,64},{128,96},{160,128},{192,160},{224,1... | collective-permute-start | bytes 835592 | tf_op jit(solution)/shard_map/ppermute | solution.py:20
  96.3 3.1 %collective-permute-start.19 = (bf16[256,2048]{1,0:T(8,128)(2,1)}, bf16[256,2048]{1,0:T(8,128)(2,1)}, u32[]{:S(2)}, u32[]{:S(2)}) collective-permute-start(bf16[256,2048]{1,0:T(8,128)(2,1)} %collective-permute-done.15.refs_15_), channel_id=1, source_target_pairs={{0,1},{1,0},{2,3},{3,2},{4,5},{5,4},{6,7},{7,6},{8,9},{9,8},{10,11... | collective-permute-start | bytes 3145736 | tf_op jit(solution)/shard_map/ppermute | solution.py:20
  96.4 4.5 %collective-permute-start.20 = (bf16[256,2048]{1,0:T(8,128)(2,1)}, bf16[256,2048]{1,0:T(8,128)(2,1)}, u32[]{:S(2)}, u32[]{:S(2)}) collective-permute-start(bf16[256,2048]{1,0:T(8,128)(2,1)} %collective-permute-done.16.refs_16_), channel_id=1, source_target_pairs={{0,1},{1,0},{2,3},{3,2},{4,5},{5,4},{6,7},{7,6},{8,9},{9,8},{10,11... | collective-permute-start | bytes 3145736 | tf_op jit(solution)/shard_map/ppermute | solution.py:20
  97.9 58.9 %copy-start.1 = (bf16[544,512]{1,0:T(8,128)(2,1)S(1)}, bf16[544,512]{1,0:T(8,128)(2,1)}, u32[]{:S(2)}) copy-start(bf16[544,512]{1,0:T(8,128)(2,1)} %copy-done) | copy-start | bytes 1671172
  97.9 58.9 %copy-start.7 = (bf16[544,512]{1,0:T(8,128)(2,1)S(1)}, bf16[544,512]{1,0:T(8,128)(2,1)}, u32[]{:S(2)}) copy-start(bf16[544,512]{1,0:T(8,128)(2,1)} %copy-done.6) | copy-start | bytes 1671172
  97.9 58.9 %copy-start.9 = (bf16[544,512]{1,0:T(8,128)(2,1)S(1)}, bf16[544,512]{1,0:T(8,128)(2,1)}, u32[]{:S(2)}) copy-start(bf16[544,512]{1,0:T(8,128)(2,1)} %copy-done.8) | copy-start | bytes 1671172
  152.4 14.9 %all-to-all-start.1 = ((bf16[32,16,128]{2,1,0:T(8,128)(2,1)}), bf16[32,16,128]{2,1,0:T(8,128)(2,1)S(1)}, u32[]{:S(2)}, u32[]{:S(2)}) async-start(bf16[32,16,128]{2,1,0:T(8,128)(2,1)} %merge.1), calls=%async_computation.1 | async-start | bytes 262144 | tf_op jit(solution)/shard_map/all_to_all | solution.py:298
  (13 other events, 64.9 us)
